TPU v7x, 1024 devices: a whole 4x8x16 slice. The times are simulated.
1024 devices in a mesh: seq: 64 (over y, x, core), head: 16 (over z).
Axes of the slice: x: 4, y: 8, z: 16, core: 2. Of those that a mesh axis runs over, the one named last changes fastest.
Arguments:
- queries: bfloat16 [16384, 8192], P('seq', 'head'), may hold values from -8 to 8
- keys: bfloat16 [16384, 2048], P('seq', 'head'), may hold values from -8 to 8
- values: bfloat16 [16384, 2048], P('seq', 'head'), may hold values from -6 to 6
- grad_out: bfloat16 [16384, 8192], P('seq', 'head'), may hold values from -6 to 6
- gate: float32 [16384, 64], P('seq', 'head'), may hold values from 0.05 to 0.95
- gate_weight: bfloat16 [64, 7168], P(None, 'head'), may hold values from -0.75 to 0.75
- selection: int32 [256, 16, 16], P(None, 'head'), may hold values from -1 to 255, as said below
Outputs:
- grad_queries: bfloat16 [16384, 8192], P('seq', 'head')
- grad_keys: bfloat16 [16384, 2048], P('seq', 'head')
- grad_values: bfloat16 [16384, 2048], P('seq', 'head')
- grad_input: bfloat16 [16384, 7168], P('seq', 'head')
Inputs may be any that keep to these rules, and one draw needn't show every extreme that they name: `selection`: row [c, g] lists distinct key blocks for query block c of group g, none after block c, always block c itself; -1 marks an unused entry, and such entries come last in a row. For one group and the 4 query blocks of one index of seq, all blocks named that lie on another index of seq are, for each such index, one and the same block.
All inputs are finite; a program needn't handle non-finite values.
Results may differ from a plain program's by a relative error of at most 0.038.
Values may be sent and summed in bfloat16 or wider, within the bound.
A program may use at most 64 MiB of HBM per device.

v0:
```python
import math

import jax
import jax.numpy as jnp
from jax import lax
from jax.sharding import PartitionSpec as P

BLK = 64


def forward_probs(query_tile, key_flat, allowed, scale):
    scores = (
        jnp.einsum("ntah,nmh->natm", query_tile, key_flat, preferred_element_type=jnp.float32)
        * scale
    )
    masked = jnp.where(allowed, scores, -jnp.inf)
    top = jnp.max(masked, axis=3)
    total = jnp.sum(jnp.exp(masked - top[..., None]), axis=3)
    lse = top + jnp.log(total)
    return jnp.exp(masked - lse[..., None])


def scatter_rows(table, rows_tile, valid_tile, term):
    width = table.shape[0]
    pairs, picks_len = rows_tile.shape
    blocked = term.reshape(pairs, picks_len, table.shape[1], table.shape[2])
    onehot = (
        (rows_tile[..., None] == jnp.arange(width, dtype=jnp.int32)) & valid_tile[..., None]
    ).astype(jnp.float32)
    return table + jnp.einsum("nsr,nskh->rkh", onehot, blocked, precision=lax.Precision.HIGHEST)


def shards(queries, keys, values, grad_out, gate, gate_weight, selection):
    tok_rows = queries.shape[0]
    head_dim = keys.shape[1]
    per_group = queries.shape[1] // head_dim
    picks_len = selection.shape[2]
    qb_dev = tok_rows // BLK
    npair = qb_dev // 2
    nseq = lax.axis_size("seq")
    me = lax.axis_index("seq")
    scale = 1.0 / math.sqrt(head_dim)
    chosen = selection[:, 0, :]
    everyone = chosen.reshape(nseq, qb_dev * picks_len)
    own_ids = me * qb_dev + jnp.arange(qb_dev, dtype=jnp.int32)
    others = jnp.arange(nseq, dtype=jnp.int32) != me
    wanted = jnp.any(everyone[:, :, None] == own_ids[None, None, :], axis=1) & others[:, None]
    request = jnp.sum(
        wanted.astype(jnp.int32) * jnp.arange(qb_dev, dtype=jnp.int32)[None, :], axis=1
    )
    key_blocks = keys.reshape(qb_dev, BLK, head_dim)
    value_blocks = values.reshape(qb_dev, BLK, head_dim)
    outgoing = (jnp.take(key_blocks, request, axis=0), jnp.take(value_blocks, request, axis=0))
    fetched_keys, fetched_values = (
        lax.all_to_all(outgoing[0], "seq", split_axis=0, concat_axis=0, tiled=True),
        lax.all_to_all(outgoing[1], "seq", split_axis=0, concat_axis=0, tiled=True),
    )
    key_table = jnp.concatenate([key_blocks, fetched_keys], axis=0)
    value_table = jnp.concatenate([value_blocks, fetched_values], axis=0)
    width = qb_dev + nseq
    mine = lax.dynamic_slice_in_dim(chosen, me * qb_dev, qb_dev, 0)
    valid = mine >= 0
    safe = jnp.where(valid, mine, 0)
    owner = safe // qb_dev
    rows = jnp.where(owner == me, safe - me * qb_dev, qb_dev + owner)
    rows = jnp.where(valid, rows, 0)
    offsets = jnp.arange(BLK, dtype=jnp.int32)
    key_pos = (safe[:, :, None] * BLK + offsets).reshape(qb_dev, picks_len * BLK)
    key_live = jnp.repeat(valid, BLK, axis=1)
    query_pos = (me * qb_dev + jnp.arange(qb_dev, dtype=jnp.int32))[:, None] * BLK + offsets
    allowed = key_live[:, None, :] & (key_pos[:, None, :] <= query_pos[:, :, None])
    tiles = (
        queries.reshape(npair, 2, BLK, per_group, head_dim),
        grad_out.reshape(npair, 2, BLK, per_group, head_dim),
        gate.reshape(npair, 2, BLK, per_group),
        rows.reshape(npair, 2, picks_len),
        valid.reshape(npair, 2, picks_len),
        allowed.reshape(npair, 2, 1, BLK, picks_len * BLK),
    )

    def forward_part(tile):
        query_tile, grad_tile, gate_tile, rows_tile, valid_tile, allowed_tile = tile
        key_flat = key_table[rows_tile].reshape(2, picks_len * BLK, head_dim)
        value_flat = value_table[rows_tile].reshape(2, picks_len * BLK, head_dim)
        probs = forward_probs(query_tile, key_flat, allowed_tile, scale)
        probs_low = probs.astype(jnp.bfloat16)
        attended = jnp.einsum(
            "natm,nmh->ntah", probs_low, value_flat, preferred_element_type=jnp.float32
        )
        grad_f = grad_tile.astype(jnp.float32)
        grad_att = (gate_tile[..., None] * grad_f).astype(jnp.bfloat16)
        gate_grad = (jnp.sum(grad_f * attended, axis=-1) * gate_tile * (1.0 - gate_tile)).astype(
            jnp.bfloat16
        )
        delta = jnp.sum(grad_att.astype(jnp.float32) * attended, axis=-1)
        value_term = jnp.einsum(
            "natm,ntah->nmh", probs_low, grad_att, preferred_element_type=jnp.float32
        )
        return (probs, grad_att, gate_grad, delta, value_term, key_flat, value_flat)

    def backward_part(tile, probs, grad_att, delta, key_flat, value_flat):
        query_tile = tile[0]
        grad_probs = jnp.einsum(
            "ntah,nmh->natm", grad_att, value_flat, preferred_element_type=jnp.float32
        )
        grad_scores = probs * (grad_probs - jnp.transpose(delta, (0, 2, 1))[..., None])
        low = grad_scores.astype(jnp.bfloat16)
        grad_query = (
            jnp.einsum("natm,nmh->ntah", low, key_flat, preferred_element_type=jnp.float32) * scale
        ).astype(jnp.bfloat16)
        key_term = (
            jnp.einsum("natm,ntah->nmh", low, query_tile, preferred_element_type=jnp.float32)
            * scale
        )
        return (grad_query, key_term)

    empty = jnp.zeros((width, BLK, head_dim), jnp.float32)

    def single_step(carry, tile):
        key_acc, value_acc = carry
        probs, grad_att, gate_grad, delta, value_term, key_flat, value_flat = forward_part(tile)
        grad_query, key_term = backward_part(tile, probs, grad_att, delta, key_flat, value_flat)
        key_acc = scatter_rows(key_acc, tile[3], tile[4], key_term)
        value_acc = scatter_rows(value_acc, tile[3], tile[4], value_term)
        return ((key_acc, value_acc), (grad_query, gate_grad))

    (key_acc, value_acc), (grad_queries, gate_grads) = lax.scan(single_step, (empty, empty), tiles)
    back_values = lax.all_to_all(value_acc[qb_dev:], "seq", split_axis=0, concat_axis=0, tiled=True)
    back_keys = lax.all_to_all(key_acc[qb_dev:], "seq", split_axis=0, concat_axis=0, tiled=True)
    wanted_f = wanted.astype(jnp.float32)
    grad_values = value_acc[:qb_dev] + jnp.einsum(
        "rj,rkh->jkh", wanted_f, back_values, precision=lax.Precision.HIGHEST
    )
    grad_keys = key_acc[:qb_dev] + jnp.einsum(
        "rj,rkh->jkh", wanted_f, back_keys, precision=lax.Precision.HIGHEST
    )
    gate_local = gate_grads.reshape(tok_rows, per_group)
    grad_input = jnp.dot(
        lax.all_gather(gate_local, "head", axis=1, tiled=True),
        gate_weight,
        preferred_element_type=jnp.float32,
    )
    return (
        grad_queries.reshape(tok_rows, per_group * head_dim),
        grad_keys.reshape(tok_rows, head_dim).astype(jnp.bfloat16),
        grad_values.reshape(tok_rows, head_dim).astype(jnp.bfloat16),
        grad_input.astype(jnp.bfloat16),
    )


def solution(mesh):
    placed = (
        P("seq", "head"),
        P("seq", "head"),
        P("seq", "head"),
        P("seq", "head"),
        P("seq", "head"),
        P(None, "head"),
        P(None, "head", None),
    )
    return jax.shard_map(
        shards,
        mesh=mesh,
        in_specs=placed,
        out_specs=(P("seq", "head"), P("seq", "head"), P("seq", "head"), P("seq", "head")),
        check_vma=False,
    )
```

profile of v0, /device:TPU:6, one launch (start us, length us, event | category | flops | bytes accessed | tf_op | source)
XLA Modules:
  0.0 246.8 jit_solution(8264706407703570676)
XLA Ops:
  0.7 0.8 copy.48
  1.5 0.1 eq.46
  1.6 0.2 compare_reduce_fusion
  1.9 1.6 gather_fusion.3
  3.5 0.7 gather_fusion.2
  4.3 1.2 broadcast_select_fusion
  5.5 46.1 %all_to_all.20 = bf16[64,64,128]{2,1,0:T(8,128)(2,1)} all-to-all(bf16[64,64,128]{2,1,0:T(8,128)(2,1)S(1)} %get-tuple-element.193), channel_id=1, replica_groups=mesh['seq'=64,'head'=16] {'seq'}, dimensions={0} | all-to-all | bytes 2097152 | tf_op jit(solution)/shard_map/all_to_all | solution.py:55
  51.6 5.8 %all-to-all-start.1 = ((bf16[64,64,128]{2,1,0:T(8,128)(2,1)}), bf16[64,64,128]{2,1,0:T(8,128)(2,1)}, u32[]{:S(2)}, u32[]{:S(2)}) async-start(bf16[64,64,128]{2,1,0:T(8,128)(2,1)} %get-tuple-element.192), calls=%async_computation.1 | async-start | bytes 2097152 | tf_op jit(solution)/shard_map/all_to_all | solution.py:56
  57.6 0.1 copy.46
  57.8 0.1 and.52
  57.9 0.1 reshape.181
  58.2 0.1 add.114
  58.5 0.2 compare_and_fusion
  58.8 2.3 pad_maximum_fusion
  61.1 25.1 %all-to-all-done.1 = bf16[64,64,128]{2,1,0:T(8,128)(2,1)} async-done(((bf16[64,64,128]{2,1,0:T(8,128)(2,1)}), bf16[64,64,128]{2,1,0:T(8,128)(2,1)}, u32[]{:S(2)}, u32[]{:S(2)}) %all-to-all-start.1) | async-done | bytes 1048608 | tf_op jit(solution)/shard_map/all_to_all | solution.py:56
  86.2 2.3 pad_maximum_fusion.1
  88.5 36.7 %while.17 = (s32[]{:T(128)}, f32[68,64,128]{2,0,1:T(8,128)}, f32[68,64,128]{2,0,1:T(8,128)S(1)}, bf16[2,2,64,4,128]{4,3,2,1,0:T(4,128)(2,1)}, bf16[2,2,64,4]{2,1...) while((s32[]{:T(128)}, f32[68,64,128]{2,0,1:T(8,128)}, ...), condition=%wide.region_7.9_spmd.clone, body=%wide.region_2.8_spmd.clone.sunk | while | flops 1243490432 | bytes 60216332 | solution.py:127
  88.6 0.1 reshape.257
  88.7 0.8 dynamic-slice_bitcast_fusion.2
  89.5 0.8 constant_dynamic-slice_fusion.8
  90.3 1.9 gather_fusion.1
  92.2 1.9 gather_fusion
  94.1 1.6 fusion.91
  95.7 0.5 exponential_reduce_fusion.2
  96.2 0.7 fusion.92
  96.9 0.6 fusion.93
  97.6 0.8 fusion.97
  98.4 0.4 fusion.98
  98.8 0.5 fusion.94
  99.4 0.1 copy_dynamic-update-slice_fusion.4
  99.5 2.9 %bitcast_add_fusion.5 = f32[68,64,128]{2,0,1:T(8,128)S(1)} fusion(f32[68,64,128]{2,0,1:T(8,128)S(1)} %get-tuple-element.302, pred[]{:T(512)S(6)} %compare.7, f32[2,16,64,128]{3,2,1,0:T(8,128)S(1)} %bitcast.191, s32[2,16]{1,0:T(2,128)S(1)} %fusion.95, pred[2,16]{1,0:T(4,128)(4,1)S(1)} %fusion.96), kind=kOutput, calls=%fused_computation.4.clone.1 | convolution fusion | flops 215027968 | bytes 5505185 | tf_op jit(solution)/shard_map/while/body/eval_jaxpr/nsr,nskh->rkh/dot_general | solution.py:30
  102.5 2.9 %bitcast_add_fusion.4 = f32[68,64,128]{2,0,1:T(8,128)S(1)} fusion(f32[68,64,128]{2,0,1:T(8,128)S(1)} %copy-done.1, pred[]{:T(512)S(6)} %compare.7, f32[2,16,64,128]{3,2,1,0:T(8,128)S(1)} %bitcast.192, s32[2,16]{1,0:T(2,128)S(1)} %fusion.95, pred[2,16]{1,0:T(4,128)(4,1)S(1)} %fusion.96), kind=kOutput, calls=%fused_computation.5.clone.1 | convolution fusion | flops 215027968 | bytes 5505185 | tf_op jit(solution)/shard_map/while/body/eval_jaxpr/nsr,nskh->rkh/dot_general | solution.py:30
  105.5 1.4 copy-done.2
  107.1 0.8 dynamic-slice_bitcast_fusion.2
  107.9 0.8 constant_dynamic-slice_fusion.8
  108.6 1.9 gather_fusion.1
  110.6 1.9 gather_fusion
  112.5 1.6 fusion.91
  114.0 0.5 exponential_reduce_fusion.2
  114.6 0.7 fusion.92
  115.3 0.6 fusion.93
  115.9 0.8 fusion.97
  116.7 0.4 fusion.98
  117.2 0.5 fusion.94
  117.8 0.1 copy_dynamic-update-slice_fusion.4
  117.9 2.9 %bitcast_add_fusion.5 = f32[68,64,128]{2,0,1:T(8,128)S(1)} fusion(f32[68,64,128]{2,0,1:T(8,128)S(1)} %get-tuple-element.302, pred[]{:T(512)S(6)} %compare.7, f32[2,16,64,128]{3,2,1,0:T(8,128)S(1)} %bitcast.191, s32[2,16]{1,0:T(2,128)S(1)} %fusion.95, pred[2,16]{1,0:T(4,128)(4,1)S(1)} %fusion.96), kind=kOutput, calls=%fused_computation.4.clone.1 | convolution fusion | flops 215027968 | bytes 5505185 | tf_op jit(solution)/shard_map/while/body/eval_jaxpr/nsr,nskh->rkh/dot_general | solution.py:30
  120.9 2.9 %bitcast_add_fusion.4 = f32[68,64,128]{2,0,1:T(8,128)S(1)} fusion(f32[68,64,128]{2,0,1:T(8,128)S(1)} %copy-done.1, pred[]{:T(512)S(6)} %compare.7, f32[2,16,64,128]{3,2,1,0:T(8,128)S(1)} %bitcast.192, s32[2,16]{1,0:T(2,128)S(1)} %fusion.95, pred[2,16]{1,0:T(4,128)(4,1)S(1)} %fusion.96), kind=kOutput, calls=%fused_computation.5.clone.1 | convolution fusion | flops 215027968 | bytes 5505185 | tf_op jit(solution)/shard_map/while/body/eval_jaxpr/nsr,nskh->rkh/dot_general | solution.py:30
  123.8 1.4 copy-done.2
  125.3 2.1 copy.53
  127.4 1.5 slice.24
  128.9 5.8 %all-to-all-start.2 = ((f32[64,64,128]{2,1,0:T(8,128)}), f32[64,64,128]{2,1,0:T(8,128)}, u32[]{:S(2)}, u32[]{:S(2)}) async-start(f32[64,64,128]{2,1,0:T(8,128)} %slice.24), calls=%async_computation.2 | async-start | bytes 4194304 | tf_op jit(solution)/shard_map/all_to_all | solution.py:129
  134.7 0.4 copy.56
  135.2 1.5 slice.25
  136.7 49.3 %all-to-all-done.2 = f32[64,64,128]{2,1,0:T(8,128)} async-done(((f32[64,64,128]{2,1,0:T(8,128)}), f32[64,64,128]{2,1,0:T(8,128)}, u32[]{:S(2)}, u32[]{:S(2)}) %all-to-all-start.2) | async-done | bytes 2097184 | tf_op jit(solution)/shard_map/all_to_all | solution.py:129
  185.9 5.6 %all-to-all-start.3 = ((f32[64,64,128]{2,1,0:T(8,128)}), f32[64,64,128]{2,1,0:T(8,128)}, u32[]{:S(2)}, u32[]{:S(2)}) async-start(f32[64,64,128]{2,1,0:T(8,128)} %slice.25), calls=%async_computation.3 | async-start | bytes 4194304 | tf_op jit(solution)/shard_map/all_to_all | solution.py:128
  191.5 0.1 reshape.184
  191.6 0.7 copy.110
  192.4 35.7 %all-gather = bf16[16,4,256]{2,1,0:T(4,128)(2,1)S(1)} all-gather(bf16[1,4,256]{2,1,0:T(4,128)(2,1)S(1)} %bitcast.212), channel_id=1, replica_groups=mesh['seq'=64,'head'=16] {'head'}, dimensions={0}, use_global_device_ids=true | all-gather | bytes 34816 | tf_op jit(solution)/shard_map/all_gather | solution.py:139
  228.1 1.0 convolution_convert_fusion
  229.0 3.4 %fusion.40 = bf16[4,64,128]{2,0,1:T(4,128)(2,1)S(1)} fusion(f32[64,64,128]{2,1,0:T(8,128)} %all-to-all-done.2, f32[68,64,128]{2,0,1:T(8,128)} %get-tuple-element.76, pred[64,4]{0,1:T(4,128)(4,1)S(1)} %compare_reduce_fusion, pred[64]{0:T(512)(128)(4,1)S(1)} %iota_compare_fusion.1), kind=kOutput, calls=%fused_computation.61 | convolution fusion | flops 25231616 | bytes 2294080 | tf_op jit(solution)/shard_map/rj,rkh->jkh/dot_general | solution.py:134
  232.5 0.6 copy.55
  233.1 9.6 %all-to-all-done.3 = f32[64,64,128]{2,1,0:T(8,128)} async-done(((f32[64,64,128]{2,1,0:T(8,128)}), f32[64,64,128]{2,1,0:T(8,128)}, u32[]{:S(2)}, u32[]{:S(2)}) %all-to-all-start.3) | async-done | bytes 2097184 | tf_op jit(solution)/shard_map/all_to_all | solution.py:128
  242.7 3.4 %fusion.37 = bf16[4,64,128]{2,0,1:T(4,128)(2,1)S(1)} fusion(f32[64,64,128]{2,1,0:T(8,128)} %all-to-all-done.3, f32[68,64,128]{2,0,1:T(8,128)S(1)} %get-tuple-element.77, pred[64,4]{0,1:T(4,128)(4,1)S(1)} %compare_reduce_fusion, pred[64]{0:T(512)(128)(4,1)S(1)} %iota_compare_fusion.1), kind=kOutput, calls=%fused_computation.60 | convolution fusion | flops 25231616 | bytes 2294080 | tf_op jit(solution)/shard_map/rj,rkh->jkh/dot_general | solution.py:131
  246.2 0.6 copy.58
  (106 shorter events, 1.0 us)
Async XLA Ops:
  0.6 227.4 %copy-start = (bf16[64,448]{1,0:T(8,128)(2,1)S(1)}, bf16[64,448]{1,0:T(8,128)(2,1)}, u32[]{:S(2)}) copy-start(bf16[64,448]{1,0:T(8,128)(2,1)} %param.16) | copy-start | bytes 172036
  0.6 2.9 %copy-start.5 = (bf16[256,128]{1,0:T(8,128)(2,1)S(1)}, bf16[256,128]{1,0:T(8,128)(2,1)}, u32[]{:S(2)}) copy-start(bf16[256,128]{1,0:T(8,128)(2,1)} %param.12) | copy-start | bytes 196612
  5.5 52.0 %copy-start.18 = (s32[256,1,16]{0,2,1:T(8,128)S(1)}, s32[256,1,16]{0,2,1:T(8,128)}, u32[]{:S(2)}) copy-start(s32[256,1,16]{0,2,1:T(8,128)} %param.17) | copy-start | bytes 49156
  5.5 52.4 %copy-start.19 = (f32[256,4]{0,1:T(4,128)S(1)}, f32[256,4]{0,1:T(4,128)}, u32[]{:S(2)}) copy-start(f32[256,4]{0,1:T(4,128)} %param.15) | copy-start | bytes 12292
  5.5 52.7 %copy-start.13 = (bf16[256,512]{1,0:T(8,128)(2,1)S(1)}, bf16[256,512]{1,0:T(8,128)(2,1)}, u32[]{:S(2)}) copy-start(bf16[256,512]{1,0:T(8,128)(2,1)} %param.11) | copy-start | bytes 786436
  5.5 52.8 %copy-start.14 = (bf16[256,512]{1,0:T(8,128)(2,1)S(1)}, bf16[256,512]{1,0:T(8,128)(2,1)}, u32[]{:S(2)}) copy-start(bf16[256,512]{1,0:T(8,128)(2,1)} %param.14) | copy-start | bytes 786436
  51.6 34.6 %all-to-all-start.1 = ((bf16[64,64,128]{2,1,0:T(8,128)(2,1)}), bf16[64,64,128]{2,1,0:T(8,128)(2,1)}, u32[]{:S(2)}, u32[]{:S(2)}) async-start(bf16[64,64,128]{2,1,0:T(8,128)(2,1)} %get-tuple-element.192), calls=%async_computation.1 | async-start | bytes 2097152 | tf_op jit(solution)/shard_map/all_to_all | solution.py:56
  57.5 28.7 %copy-start.6 = (bf16[256,128]{1,0:T(8,128)(2,1)S(1)}, bf16[256,128]{1,0:T(8,128)(2,1)}, u32[]{:S(2)}) copy-start(bf16[256,128]{1,0:T(8,128)(2,1)} %param.13) | copy-start | bytes 196612
  88.5 1.7 copy-start.9
  88.5 1.7 copy-start.11
  88.5 3.6 %copy-start.7 = (bf16[2,2,64,4,128]{4,3,2,1,0:T(4,128)(2,1)}, bf16[2,2,64,4,128]{4,3,2,1,0:T(4,128)(2,1)S(1)}, u32[]{:S(2)}) copy-start(bf16[2,2,64,4,128]{4,3,2,1,0:T(4,128)(2,1)S(1)} %get-tuple-element.324) | copy-start | bytes 786436 | tf_op jit(solution)/shard_map/while
  94.1 2.1 copy-start.3
  97.5 1.3 copy-start.4
  98.4 1.0 copy-start.15
  99.5 3.0 %copy-start.16 = (bf16[2,2,64,4,128]{4,3,2,1,0:T(4,128)(2,1)}, bf16[2,2,64,4,128]{4,3,2,1,0:T(4,128)(2,1)S(1)}, u32[]{:S(2)}) copy-start(bf16[2,2,64,4,128]{4,3,2,1,0:T(4,128)(2,1)S(1)} %copy_dynamic-update-slice_fusion.4) | copy-start | bytes 786436 | tf_op jit(solution)/shard_map/while
  99.5 3.0 %copy-start.1 = (f32[68,64,128]{2,0,1:T(8,128)S(1)}, f32[68,64,128]{2,0,1:T(8,128)}, u32[]{:S(2)}) copy-start(f32[68,64,128]{2,0,1:T(8,128)} %get-tuple-element.301) | copy-start | bytes 6684676 | tf_op jit(solution)/shard_map/while
  102.5 4.4 %copy-start.8 = (bf16[2,2,64,4,128]{4,3,2,1,0:T(4,128)(2,1)S(1)}, bf16[2,2,64,4,128]{4,3,2,1,0:T(4,128)(2,1)}, u32[]{:S(2)}) copy-start(bf16[2,2,64,4,128]{4,3,2,1,0:T(4,128)(2,1)} %copy-done.7) | copy-start | bytes 786436 | tf_op jit(solution)/shard_map/while
  102.5 4.4 %copy-start.10 = (bf16[2,2,64,4,128]{4,3,2,1,0:T(4,128)(2,1)S(1)}, bf16[2,2,64,4,128]{4,3,2,1,0:T(4,128)(2,1)}, u32[]{:S(2)}) copy-start(bf16[2,2,64,4,128]{4,3,2,1,0:T(4,128)(2,1)} %copy-done.9) | copy-start | bytes 786436 | tf_op jit(solution)/shard_map/while
  102.5 4.4 %copy-start.12 = (pred[2,2,1,64,1024]{4,3,1,2,0:T(8,128)(4,1)S(1)}, pred[2,2,1,64,1024]{4,3,1,2,0:T(8,128)(4,1)}, u32[]{:S(2)}) copy-start(pred[2,2,1,64,1024]{4,3,1,2,0:T(8,128)(4,1)} %copy-done.11) | copy-start | bytes 786436 | tf_op jit(solution)/shard_map/while
  105.5 1.4 copy-start.2
  106.9 1.7 copy-start.9
  106.9 1.7 copy-start.11
  106.9 3.6 %copy-start.7 = (bf16[2,2,64,4,128]{4,3,2,1,0:T(4,128)(2,1)}, bf16[2,2,64,4,128]{4,3,2,1,0:T(4,128)(2,1)S(1)}, u32[]{:S(2)}) copy-start(bf16[2,2,64,4,128]{4,3,2,1,0:T(4,128)(2,1)S(1)} %get-tuple-element.324) | copy-start | bytes 786436 | tf_op jit(solution)/shard_map/while
  112.5 2.1 copy-start.3
  115.9 1.3 copy-start.4
  116.7 1.0 copy-start.15
  117.9 3.0 %copy-start.16 = (bf16[2,2,64,4,128]{4,3,2,1,0:T(4,128)(2,1)}, bf16[2,2,64,4,128]{4,3,2,1,0:T(4,128)(2,1)S(1)}, u32[]{:S(2)}) copy-start(bf16[2,2,64,4,128]{4,3,2,1,0:T(4,128)(2,1)S(1)} %copy_dynamic-update-slice_fusion.4) | copy-start | bytes 786436 | tf_op jit(solution)/shard_map/while
  117.9 3.0 %copy-start.1 = (f32[68,64,128]{2,0,1:T(8,128)S(1)}, f32[68,64,128]{2,0,1:T(8,128)}, u32[]{:S(2)}) copy-start(f32[68,64,128]{2,0,1:T(8,128)} %get-tuple-element.301) | copy-start | bytes 6684676 | tf_op jit(solution)/shard_map/while
  120.9 4.4 %copy-start.8 = (bf16[2,2,64,4,128]{4,3,2,1,0:T(4,128)(2,1)S(1)}, bf16[2,2,64,4,128]{4,3,2,1,0:T(4,128)(2,1)}, u32[]{:S(2)}) copy-start(bf16[2,2,64,4,128]{4,3,2,1,0:T(4,128)(2,1)} %copy-done.7) | copy-start | bytes 786436 | tf_op jit(solution)/shard_map/while
  120.9 4.4 %copy-start.10 = (bf16[2,2,64,4,128]{4,3,2,1,0:T(4,128)(2,1)S(1)}, bf16[2,2,64,4,128]{4,3,2,1,0:T(4,128)(2,1)}, u32[]{:S(2)}) copy-start(bf16[2,2,64,4,128]{4,3,2,1,0:T(4,128)(2,1)} %copy-done.9) | copy-start | bytes 786436 | tf_op jit(solution)/shard_map/while
  120.9 4.4 %copy-start.12 = (pred[2,2,1,64,1024]{4,3,1,2,0:T(8,128)(4,1)S(1)}, pred[2,2,1,64,1024]{4,3,1,2,0:T(8,128)(4,1)}, u32[]{:S(2)}) copy-start(pred[2,2,1,64,1024]{4,3,1,2,0:T(8,128)(4,1)} %copy-done.11) | copy-start | bytes 786436 | tf_op jit(solution)/shard_map/while
  123.8 1.4 copy-start.2
  128.9 57.0 %all-to-all-start.2 = ((f32[64,64,128]{2,1,0:T(8,128)}), f32[64,64,128]{2,1,0:T(8,128)}, u32[]{:S(2)}, u32[]{:S(2)}) async-start(f32[64,64,128]{2,1,0:T(8,128)} %slice.24), calls=%async_computation.2 | async-start | bytes 4194304 | tf_op jit(solution)/shard_map/all_to_all | solution.py:129
  136.7 54.9 %copy-start.17 = (bf16[2,2,64,4,128]{4,3,2,1,0:T(4,128)(2,1)S(1)}, bf16[2,2,64,4,128]{4,3,2,1,0:T(4,128)(2,1)}, u32[]{:S(2)}) copy-start(bf16[2,2,64,4,128]{4,3,2,1,0:T(4,128)(2,1)} %get-tuple-element.75) | copy-start | bytes 786436
  185.9 56.8 %all-to-all-start.3 = ((f32[64,64,128]{2,1,0:T(8,128)}), f32[64,64,128]{2,1,0:T(8,128)}, u32[]{:S(2)}, u32[]{:S(2)}) async-start(f32[64,64,128]{2,1,0:T(8,128)} %slice.25), calls=%async_computation.3 | async-start | bytes 4194304 | tf_op jit(solution)/shard_map/all_to_all | solution.py:128
where the time goes:
time: 248 us; the launch traced here: 247 us
  waiting for transfers between devices  84 us (34%)
  blocking collectives  81.8 us (33%)
  matrix products  28.8 us (12%)
  local copies, waits for them, and re-layouts  25.9 us (10%)
  starting transfers between devices  17.3 us (7%)
  other arithmetic  7.64 us (3%)
    all_to_all x1, waiting for transfers between devices, shards(): lax.all_to_all(key_acc[qb_dev:], 'seq', split_axis=0, concat_axis=0, tile...  49.3 us
    all_to_all x1, blocking collectives, shards(): lax.all_to_all(outgoing[0], 'seq', split_axis=0, concat_axis=0, tiled=True)  46.1 us
    all_gather x1, blocking collectives, shards(): lax.all_gather(gate_local, 'head', axis=1, tiled=True)  35.7 us
    all_to_all x1, waiting for transfers between devices, shards(): lax.all_to_all(outgoing[1], 'seq', split_axis=0, concat_axis=0, tiled=True)  25.1 us
    dot_general x4, matrix products, scatter_rows(): jnp.einsum('nsr,nskh->rkh', onehot, blocked, precision=lax.Precision.HIGH...  11.7 us
    all_to_all x1, waiting for transfers between devices, shards(): lax.all_to_all(value_acc[qb_dev:], 'seq', split_axis=0, concat_axis=0, ti...  9.62 us
    all_to_all x1, starting transfers between devices, shards(): lax.all_to_all(outgoing[1], 'seq', split_axis=0, concat_axis=0, tiled=True)  5.84 us
    all_to_all x1, starting transfers between devices, shards(): lax.all_to_all(key_acc[qb_dev:], 'seq', split_axis=0, concat_axis=0, tile...  5.84 us
  transfers between devices with their start and end apart: 3, of which 3 were waited for; matrix products, arithmetic and copies ran while one was open for 5% of the time, Pallas kernels for 0%

commit v1 on v0

v1 whole, which is shorter than its diff:
```python
import functools
import math

import jax
import jax.numpy as jnp
from jax import lax
from jax.experimental import pallas as pl
from jax.experimental.pallas import tpu as pltpu
from jax.sharding import PartitionSpec as P

BLK = 64
HD = 128
QB = 4
SEL = 16
GQA = 4
NY = 8
NW = 8
NZ = 16
NSEQ = NY * NW
MESH = pl.DeviceIdType.MESH
SCALE = 1.0 / math.sqrt(HD)
EXP2_SCALE = SCALE / math.log(2.0)


def dot(a, b, dims):
    return lax.dot_general(a, b, (dims, ((), ())), preferred_element_type=jnp.float32)


NN = ((1,), (0,))
NT = ((1,), (1,))
TN = ((0,), (0,))


def kernel(
    q_ref, k_ref, v_ref, g_ref, gate_ref, gw_ref, slot_ref, count_ref, pos_ref, req_ref,
    dq_ref, dk_ref, dv_ref, gi_ref,
    col0, col1, col2, col3, col4, col5, col6, col7,
    stage, tab, kc, vc, terms_k, terms_v, gg, gs, gbuf, gwp,
    snd, rx, dn_out, dn_in, up_out, up_in,
    f_s, f_r, b_s, b_r, x_s, x_r, y_s, y_r, dn_s, dn_r, up_s, up_r, g_s, g_r,
):
    cols = (col0, col1, col2, col3, col4, col5, col6, col7)
    s = lax.axis_index("seq")
    z = lax.axis_index("head")
    y = s // NW
    w = lax.rem(s, NW)

    def mate(m):
        return (y * NW + lax.rem(w + m, NW), z)

    def row_of(r):
        return lax.rem(y + (NY - r), NY)

    above = (lax.rem(y + 1, NY) * NW + w, z)
    below = (lax.rem(y + NY - 1, NY) * NW + w, z)

    def zmate(m):
        return (s, lax.rem(z + m, NZ))

    barrier = pltpu.get_barrier_semaphore()
    for m in range(1, NW):
        pl.semaphore_signal(barrier, inc=1, device_id=mate(m), device_id_type=MESH)
    pl.semaphore_signal(barrier, inc=1, device_id=above, device_id_type=MESH)
    pl.semaphore_signal(barrier, inc=1, device_id=below, device_id_type=MESH)
    for m in range(1, NZ):
        pl.semaphore_signal(barrier, inc=1, device_id=zmate(m), device_id_type=MESH)
    own_k = k_ref[...].reshape(QB, BLK, HD)
    own_v = v_ref[...].reshape(QB, BLK, HD)
    cols[0][0] = own_k
    cols[0][1] = own_v
    tab[NSEQ:, 0] = own_k
    tab[NSEQ:, 1] = own_v
    pl.semaphore_wait(barrier, NW + NZ)

    def copy(src, dst, send, recv, to):
        return pltpu.make_async_remote_copy(
            src_ref=src, dst_ref=dst, send_sem=send, recv_sem=recv, device_id=to, device_id_type=MESH
        )

    def ring_up(k):
        return copy(cols[k], cols[k + 1], f_s.at[k], f_r.at[k], above)

    def ring_down(k):
        return copy(cols[(NY - k) % NY], cols[NY - 1 - k], b_s.at[k], b_r.at[k], below)

    def fetch(r, m):
        return copy(stage.at[r, m], tab.at[row_of(r) * NW + w], x_s.at[r, m], x_r.at[r, m], mate(m))

    def arrive(r, m):
        owner = row_of(r) * NW + lax.rem(w + NW - m, NW)
        return copy(stage.at[r, m], tab.at[owner], x_s.at[r, m], x_r.at[r, m], mate(m))

    def hand_out(r):
        owner = row_of(r) * NW + w
        tab[owner] = cols[r][:, jnp.maximum(req_ref[w, owner], 0)]

        def one(m, c):
            block = jnp.maximum(req_ref[lax.rem(w + m, NW), owner], 0)
            stage[r, m] = cols[r][:, block]
            fetch(r, m).start()
            return c

        lax.fori_loop(1, NW, one, 0)

    ring_up(0).start()
    ring_down(0).start()
    hand_out(0)
    for k in range(4):
        ring_up(k).wait_recv()
        if k < 3:
            ring_up(k + 1).start()
        hand_out(k + 1)
        if k < 3:
            ring_down(k).wait_recv()
            if k < 2:
                ring_down(k + 1).start()
            hand_out(NY - 1 - k)

    for r in range(NY):

        def landed(m, c, r=r):
            arrive(r, m).wait_recv()
            return c

        lax.fori_loop(1, NW, landed, 0)

    none = jnp.zeros((BLK, HD), jnp.float32)
    for q in range(QB):
        terms_k[q, SEL] = none
        terms_v[q, SEL] = none

    def attend(q, c):
        rows = pl.ds(pl.multiple_of(q * BLK, BLK), BLK)
        lanes = [slice(h * HD, (h + 1) * HD) for h in range(GQA)]
        qc = jnp.concatenate([q_ref[rows, a] for a in lanes], axis=0)
        gf = jnp.concatenate([g_ref[rows, a] for a in lanes], axis=0).astype(jnp.float32)
        gate = gate_ref[rows, :]
        gate_c = jnp.concatenate(
            [jnp.broadcast_to(gate[:, h : h + 1], (BLK, HD)) for h in range(GQA)], axis=0
        )
        da = (gate_c * gf).astype(jnp.bfloat16)
        for p in range(SEL):
            at = slot_ref[q, p]
            kc[p * BLK : (p + 1) * BLK] = tab[at, 0]
            vc[p * BLK : (p + 1) * BLK] = tab[at, 1]
        keys = kc[...]
        vals = vc[...]
        st = dot(keys, qc, NT)
        u = lax.broadcasted_iota(jnp.int32, (BLK, GQA * BLK), 0)
        t = lax.rem(lax.broadcasted_iota(jnp.int32, (BLK, GQA * BLK), 1), BLK)
        first = jnp.where(u <= t, st[:BLK], -jnp.inf)
        at = lax.broadcasted_iota(jnp.int32, ((SEL - 1) * BLK, GQA * BLK), 0)
        rest = jnp.where(at < (count_ref[q] - 1) * BLK, st[BLK:], -jnp.inf)
        st = jnp.concatenate([first, rest], axis=0)
        top = jnp.max(st, axis=0, keepdims=True)
        e = jnp.exp2((st - top) * EXP2_SCALE)
        probs = e * (1.0 / jnp.sum(e, axis=0, keepdims=True))
        low = probs.astype(jnp.bfloat16)
        att_t = dot(vals, low, TN)
        g_t = gf.T
        gate_t = gate_c.T
        da_t = (gate_t * g_t).astype(jnp.bfloat16).astype(jnp.float32)
        gate_row = gate_t[:1]
        gsum = jnp.sum(g_t * att_t, axis=0, keepdims=True)
        ggrad = (gsum * gate_row * (1.0 - gate_row)).astype(jnp.bfloat16).astype(jnp.float32)
        gg[pl.ds(q, 1), :] = ggrad
        delta = jnp.sum(da_t * att_t, axis=0, keepdims=True)
        dp = dot(vals, da, NT)
        ds = (probs * (dp - delta)).astype(jnp.bfloat16)
        terms_v[q, :SEL] = dot(low, da, NN).reshape(SEL, BLK, HD)
        terms_k[q, :SEL] = (dot(ds, qc, NN) * SCALE).reshape(SEL, BLK, HD)
        dq = (dot(keys, ds, TN) * SCALE).T.astype(jnp.bfloat16)
        for h in range(GQA):
            dq_ref[rows, lanes[h]] = dq[h * BLK : (h + 1) * BLK]
        return c

    lax.fori_loop(0, QB, attend, 0)

    gs[...] = jnp.zeros_like(gs)
    for q in range(QB):
        for h in range(GQA):
            gs[h : h + 1, q * BLK : (q + 1) * BLK] = gg[q : q + 1, h * BLK : (h + 1) * BLK]
    gbuf[z] = gs[...]

    def gate_out(m):
        return copy(gs, gbuf.at[z], g_s.at[m], g_r.at[m], zmate(m))

    def gate_in(m):
        return copy(gs, gbuf.at[lax.rem(z + NZ - m, NZ)], g_s.at[m], g_r.at[m], zmate(m))

    def gate_start(m, c):
        gate_out(m).start()
        return c

    lax.fori_loop(1, NZ, gate_start, 0)

    def give(r, m):
        return copy(snd.at[r, m], rx.at[r, m], y_s.at[r, m], y_r.at[r, m], mate(m))

    def summed(slot):
        total_k = terms_k[0, pos_ref[0, slot]]
        total_v = terms_v[0, pos_ref[0, slot]]
        for q in range(1, QB):
            at = pos_ref[q, slot]
            total_k = total_k + terms_k[q, at]
            total_v = total_v + terms_v[q, at]
        return total_k, total_v

    def send_row(r):
        def one(i, c):
            m = lax.rem(i, NW)
            total_k, total_v = summed(row_of(r) * NW + lax.rem(w + m, NW))
            snd[r, m, 0] = total_k.astype(jnp.bfloat16)
            snd[r, m, 1] = total_v.astype(jnp.bfloat16)

            @pl.when(m > 0)
            def _():
                give(r, m).start()

            return c

        lax.fori_loop(1, NW + 1, one, 0)

    order = (4, 5, 3, 6, 2, 7, 1, 0)
    for r in order:
        send_row(r)

    gwp[...] = jnp.zeros_like(gwp)
    gw = gw_ref[...].astype(jnp.float32)
    for i in range(NZ):
        gwp[8 * i : 8 * i + GQA] = gw[GQA * i : GQA * (i + 1)]

    def reduced(r):
        def wait(m, c):
            give(r, m).wait_recv()
            return c

        lax.fori_loop(1, NW, wait, 0)
        owner = row_of(r) * NW + w
        out = []
        for t in range(2):
            totals = [None] * QB
            for m in range(NW):
                val = (snd[r, 0, t] if m == 0 else rx[r, m, t]).astype(jnp.float32)
                asked = req_ref[lax.rem(w + NW - m, NW), owner]
                for j in range(QB):
                    part = jnp.where(asked == j, val, 0.0)
                    totals[j] = part if m == 0 else totals[j] + part
            out.append(totals)
        return out

    def down(k):
        return copy(dn_out.at[k], dn_in.at[k - 1], dn_s.at[k], dn_r.at[k], below)

    def up(k):
        return copy(up_out.at[k], up_in.at[k - 1], up_s.at[k], up_r.at[k], above)

    for r in order[:-1]:
        if r == 1:
            def gate_wait(m, c):
                gate_in(m).wait_recv()
                return c

            lax.fori_loop(1, NZ, gate_wait, 0)
            gates = gbuf[...].reshape(NZ * 8, QB * BLK).astype(jnp.bfloat16)
            gi_ref[...] = dot(gates, gwp[...].astype(jnp.bfloat16), TN).astype(jnp.bfloat16)
        totals = reduced(r)
        if r <= 4:
            k, inn, out, hop, last = r, dn_in, dn_out, down, 4
        else:
            k, inn, out, hop, last = NY - r, up_in, up_out, up, 3
        if k < last:
            hop(k + 1).wait_recv()
        for t in range(2):
            for j in range(QB):
                val = totals[t][j]
                if k < last:
                    val = val + inn[k, t, j].astype(jnp.float32)
                out[k, t, j] = val.astype(jnp.bfloat16)
        hop(k).start()

    totals = reduced(0)
    down(1).wait_recv()
    up(1).wait_recv()
    for j in range(QB):
        own = summed(NSEQ + j)
        for t, ref in ((0, dk_ref), (1, dv_ref)):
            val = totals[t][j] + own[t]
            val = val + dn_in[0, t, j].astype(jnp.float32) + up_in[0, t, j].astype(jnp.float32)
            ref[j * BLK : (j + 1) * BLK] = val.astype(jnp.bfloat16)

    for k in range(4):
        ring_up(k).wait_send()
        down(k + 1).wait_send()
    for k in range(3):
        ring_down(k).wait_send()
        up(k + 1).wait_send()
    for r in range(NY):

        def sent(m, c, r=r):
            fetch(r, m).wait_send()
            give(r, m).wait_send()
            return c

        lax.fori_loop(1, NW, sent, 0)

    def gate_sent(m, c):
        gate_out(m).wait_send()
        return c

    lax.fori_loop(1, NZ, gate_sent, 0)


def shards(queries, keys, values, grad_out, gate, gate_weight, selection):
    me = lax.axis_index("seq")
    chosen = selection[:, 0, :]
    mine = lax.dynamic_slice_in_dim(chosen, me * QB, QB, 0)
    own = me * QB + jnp.arange(QB, dtype=jnp.int32)[:, None]
    picks = jnp.arange(SEL, dtype=jnp.int32)[None, :]
    ordered = jnp.where(picks == 0, own, jnp.where(mine == own, mine[:, :1], mine))
    valid = ordered >= 0
    owner = ordered // QB
    slot = jnp.where(owner == me, NSEQ + ordered - me * QB, owner)
    slot = jnp.where(valid, slot, NSEQ + own - me * QB)
    count = jnp.sum(valid.astype(jnp.int32), axis=1)
    slots = jnp.arange(NSEQ + QB, dtype=jnp.int32)
    hit = (slot[:, :, None] == slots) & valid[:, :, None]
    pos = jnp.min(jnp.where(hit, picks[:, :, None], SEL), axis=1)
    row = lax.dynamic_slice_in_dim(chosen, me // NW * NW * QB, NW * QB, 0).reshape(NW, QB * SEL)
    owners = jnp.arange(NSEQ, dtype=jnp.int32)
    named = (row // QB)[:, :, None] == owners
    req = jnp.max(jnp.where(named, lax.rem(row, QB)[:, :, None], -1), axis=1)

    vmem = pl.BlockSpec(memory_space=pltpu.VMEM)
    smem = pl.BlockSpec(memory_space=pltpu.SMEM)
    bf, f32 = jnp.bfloat16, jnp.float32
    dma = pltpu.SemaphoreType.DMA
    pair = (2, QB, BLK, HD)
    return pl.pallas_call(
        kernel,
        out_shape=(
            jax.ShapeDtypeStruct(queries.shape, bf),
            jax.ShapeDtypeStruct(keys.shape, bf),
            jax.ShapeDtypeStruct(values.shape, bf),
            jax.ShapeDtypeStruct((queries.shape[0], gate_weight.shape[1]), bf),
        ),
        in_specs=[vmem] * 6 + [smem] * 4,
        out_specs=(vmem,) * 4,
        scratch_shapes=[pltpu.VMEM(pair, bf) for _ in range(NY)]
        + [
            pltpu.VMEM((NY, NW, 2, BLK, HD), bf),
            pltpu.VMEM((NSEQ + QB, 2, BLK, HD), bf),
            pltpu.VMEM((SEL * BLK, HD), bf),
            pltpu.VMEM((SEL * BLK, HD), bf),
            pltpu.VMEM((QB, SEL + 1, BLK, HD), f32),
            pltpu.VMEM((QB, SEL + 1, BLK, HD), f32),
            pltpu.VMEM((8, GQA * BLK), f32),
            pltpu.VMEM((8, QB * BLK), f32),
            pltpu.VMEM((NZ, 8, QB * BLK), f32),
            pltpu.VMEM((NZ * 8, gate_weight.shape[1]), f32),
            pltpu.VMEM((NY, NW, 2, BLK, HD), bf),
            pltpu.VMEM((NY, NW, 2, BLK, HD), bf),
            pltpu.VMEM((5,) + pair, bf),
            pltpu.VMEM((4,) + pair, bf),
            pltpu.VMEM((4,) + pair, bf),
            pltpu.VMEM((3,) + pair, bf),
            dma((4,)), dma((4,)), dma((3,)), dma((3,)),
            dma((NY, NW)), dma((NY, NW)), dma((NY, NW)), dma((NY, NW)),
            dma((5,)), dma((5,)), dma((4,)), dma((4,)),
            dma((NZ,)), dma((NZ,)),
        ],
        compiler_params=pltpu.CompilerParams(
            collective_id=0, has_side_effects=True, vmem_limit_bytes=56 << 20
        ),
    )(queries, keys, values, grad_out, gate, gate_weight, slot, count, pos, req)


def solution(mesh):
    placed = (
        P("seq", "head"),
        P("seq", "head"),
        P("seq", "head"),
        P("seq", "head"),
        P("seq", "head"),
        P(None, "head"),
        P(None, "head", None),
    )
    return jax.shard_map(
        shards,
        mesh=mesh,
        in_specs=placed,
        out_specs=(P("seq", "head"), P("seq", "head"), P("seq", "head"), P("seq", "head")),
        check_vma=False,
    )
```

time: 248 us -> 95.4 us (0.38)
  the two profiles are of different devices: /device:TPU:6 before, /device:TPU:1 now
where the time goes in v1:
time: 95.4 us; the launch traced here: 95.1 us
  Pallas kernels  85.9 us (90%)
  local copies, waits for them, and re-layouts  6.15 us (6%)
  other arithmetic  2.31 us (2%)
    pallas_call x1, Pallas kernels, shards(): pl.pallas_call(kernel, out_shape=(jax.ShapeDtypeStruct(queries.shape, bf)...  85.9 us
    unnamed x16, local copies, waits for them, and re-layouts  3.84 us

profile of v1, /device:TPU:1, one launch (start us, length us, event | category | flops | bytes accessed | tf_op | source)
XLA Modules:
  0.0 95.1 jit_solution(8803738742777575247)
XLA Ops:
  0.6 0.0 copy-start
  0.7 0.7 copy-done
  1.4 0.1 constant_dynamic-slice_fusion
  1.4 0.1 constant_dynamic-slice_fusion.1
  1.5 0.1 copy.18
  1.6 0.1 slice_reduce_fusion
  1.7 0.7 convert_reduce_fusion
  2.4 0.1 fusion.4.slot_ref
  2.5 0.0 copy-start.4
  2.5 0.7 select_reduce_fusion.1.pos_ref
  3.2 0.0 copy-done.4
  3.2 0.1 copy.19
  3.3 0.1 reshape.226
  3.4 0.0 copy-start.5
  3.4 0.8 select_reduce_fusion.req_ref
  4.2 0.0 copy-done.5
  4.2 0.8 copy.20.gate_ref
  5.0 85.9 %shard_map.102 = (bf16[256,512]{1,0:T(8,128)(2,1)}, bf16[256,128]{1,0:T(8,128)(2,1)}, bf16[256,128]{1,0:T(8,128)(2,1)}, bf16[256,448]{1,0:T(8,128)(2,1)}) custom-call(bf16[256,512]{1,0:T(8,128)(2,1)} %q_ref.1, bf16[256,128]{1,0:T(8,128)(2,1)} %k_ref.1, bf16[256,128]{1,0:T(8,128)(2,1)} %v_ref.1, bf16[256,512]{1,0:T(8,128)(2,1)} %g_ref.1, ...), custom_call_target="tpu_custom_call" | custom-call | tf_op jit(solution)/shard_map/pallas_call | solution.py:339
  90.9 0.0 copy-start.1
  90.9 1.8 %copy.21 = bf16[256,448]{0,1:T(8,128)(2,1)} copy(bf16[256,448]{1,0:T(8,128)(2,1)} %get-tuple-element.15) | data formatting | bytes 458752 | tf_op jit(solution)/shard_map/pallas_call | solution.py:339
  92.7 0.0 copy-done.1
  92.7 0.0 copy-start.3
  92.7 0.7 copy.25
  93.4 0.2 copy-done.3
  93.6 0.0 copy-start.2
  93.6 0.6 copy.26
  94.2 0.2 copy-done.2
  94.4 0.6 copy.27
  (3 shorter events, 0.0 us)
Async XLA Ops:
  0.6 0.7 copy-start
  2.5 0.7 copy-start.4
  3.4 0.8 copy-start.5
  90.9 1.8 %copy-start.1 = (bf16[256,512]{1,0:T(8,128)(2,1)S(1)}, bf16[256,512]{1,0:T(8,128)(2,1)}, u32[]{:S(2)}) copy-start(bf16[256,512]{1,0:T(8,128)(2,1)} %get-tuple-element.26) | copy-start | bytes 786436
  92.7 0.9 copy-start.3
  93.6 0.9 copy-start.2

commit v2 on v0

v2 whole, which is shorter than its diff:
```python
import functools
import math

import jax
import jax.numpy as jnp
from jax import lax
from jax.experimental import pallas as pl
from jax.experimental.pallas import tpu as pltpu
from jax.sharding import PartitionSpec as P

BLK = 64
HD = 128
QB = 4
SEL = 16
GQA = 4
NY = 8
NW = 8
NZ = 16
NSEQ = NY * NW
MESH = pl.DeviceIdType.MESH
SCALE = 1.0 / math.sqrt(HD)
EXP2_SCALE = SCALE / math.log(2.0)


def dot(a, b, dims):
    return lax.dot_general(a, b, (dims, ((), ())), preferred_element_type=jnp.float32)


NN = ((1,), (0,))
NT = ((1,), (1,))
TN = ((0,), (0,))


def kernel(
    q_hbm, k_hbm, v_hbm, g_hbm, gate_hbm, gw_hbm, sel_hbm,
    dq_hbm, dk_ref, dv_ref, gi_hbm,
    *scratch,
):
    cols = (scratch[:NY], scratch[NY : 2 * NY])
    (
        q_ref, g_ref, gate_ref, gw_ref, sel_ref, dq_ref, gi_ref,
        tbl, req_s, code_s, pos_s,
        stage, tab_k, tab_v, kc, vc, probs_ref, qc_ref, da_ref, terms_k, terms_v,
        gr, gg, gbuf, gwp, snd, rx, dn_out, dn_in, up_out, up_in,
        in_s, out_s, t_s, f_s, f_r, b_s, b_r, x_s, x_r, y_s, y_r, dn_s, dn_r, up_s, up_r, gu_s, gu_r, gd_s, gd_r,
    ) = scratch[2 * NY :]
    tab = (tab_k, tab_v)
    terms = (terms_k, terms_v)
    s = lax.axis_index("seq")
    z = lax.axis_index("head")
    y = s // NW
    w = lax.rem(s, NW)

    def mate(m):
        return (y * NW + lax.rem(w + m, NW), z)

    def row_of(r):
        return lax.rem(y + (NY - r), NY)

    above = (lax.rem(y + 1, NY) * NW + w, z)
    below = (lax.rem(y + NY - 1, NY) * NW + w, z)
    ahead = [(s, lax.rem(z + i, NZ)) for i in (1, 2)]
    behind = [(s, lax.rem(z + NZ - i, NZ)) for i in (1, 2)]

    barrier = pltpu.get_barrier_semaphore()
    for m in range(1, NW):
        pl.semaphore_signal(barrier, inc=1, device_id=mate(m), device_id_type=MESH)
    for to in (above, below, *ahead, *behind):
        pl.semaphore_signal(barrier, inc=1, device_id=to, device_id_type=MESH)

    loads = [
        pltpu.make_async_copy(a, b, in_s.at[i])
        for i, (a, b) in enumerate(
            (
                (k_hbm, cols[0][0]), (v_hbm, cols[1][0]), (sel_hbm, sel_ref),
                (k_hbm, tab_k.at[pl.ds(NSEQ, QB)]), (v_hbm, tab_v.at[pl.ds(NSEQ, QB)]),
                (gate_hbm, gate_ref), (g_hbm, g_ref), (q_hbm, q_ref), (gw_hbm, gw_ref),
            )
        )
    ]
    for load in loads:
        load.start()

    loads[2].wait()
    sel = sel_ref[...]
    owner = jnp.right_shift(sel, 2)
    inner = jnp.bitwise_and(sel, 3)
    code = jnp.where(owner == s, NSEQ + inner, owner)
    mine = lax.broadcasted_iota(jnp.int32, (NY, NSEQ * QB), 0) * NW + w
    slots = lax.broadcasted_iota(jnp.int32, (NSEQ + 8, NSEQ * QB), 0)
    req = jnp.full((NY, NSEQ * QB), -1, jnp.int32)
    for p in range(SEL):
        req = jnp.where(owner[p : p + 1] == mine, inner[p : p + 1], req)
    tbl[0:NY] = req
    half = pl.ds(pl.multiple_of(y // 4 * HD, HD), HD)
    req_in = pltpu.make_async_copy(tbl.at[pl.ds(0, NY), half], req_s, t_s.at[0])
    req_in.start()
    pos = jnp.full((NSEQ + 8, NSEQ * QB), SEL, jnp.int32)
    for p in range(SEL):
        pos = jnp.where(code[p : p + 1] == slots, p, pos)
    tbl[NY : NY + SEL] = code
    tbl[NY + SEL :] = pos
    code_in = pltpu.make_async_copy(tbl.at[pl.ds(NY, SEL), half], code_s, t_s.at[1])
    pos_in = pltpu.make_async_copy(tbl.at[pl.ds(NY + SEL, NSEQ + 8), half], pos_s, t_s.at[2])
    code_in.start()
    pos_in.start()
    row_lane = lax.rem(y, 4) * (NW * QB)
    lane = row_lane + w * QB

    def asked(r, d):
        at = row_lane + d * QB
        got = req_s[row_of(r), at]
        for q in range(1, QB):
            got = jnp.maximum(got, req_s[row_of(r), at + q])
        return got

    loads[0].wait()
    loads[1].wait()
    pl.semaphore_wait(barrier, NW + 5)

    def copy(src, dst, send, recv, to):
        return pltpu.make_async_remote_copy(
            src_ref=src, dst_ref=dst, send_sem=send, recv_sem=recv, device_id=to, device_id_type=MESH
        )

    def ring_up(t, k):
        return copy(cols[t][k], cols[t][k + 1], f_s.at[t, k], f_r.at[t, k], above)

    def ring_down(t, k):
        return copy(cols[t][(NY - k) % NY], cols[t][NY - 1 - k], b_s.at[t, k], b_r.at[t, k], below)

    def fetch(t, r, m):
        return copy(stage.at[t, r, m], tab[t].at[row_of(r) * NW + w], x_s.at[t, r, m], x_r.at[t, r, m], mate(m))

    def arrive(t, r, m):
        home = row_of(r) * NW + lax.rem(w + NW - m, NW)
        return copy(stage.at[t, r, m], tab[t].at[home], x_s.at[t, r, m], x_r.at[t, r, m], mate(m))

    def hand_out(t, r):
        tab[t][row_of(r) * NW + w] = cols[t][r][jnp.maximum(asked(r, w), 0)]

        def one(m, c):
            block = jnp.maximum(asked(r, lax.rem(w + m, NW)), 0)
            stage[t, r, m] = cols[t][r][block]
            fetch(t, r, m).start()
            return c

        lax.fori_loop(1, NW, one, 0)

    for t in range(2):
        ring_up(t, 0).start()
        ring_down(t, 0).start()
    req_in.wait()
    hand_out(0, 0)
    hand_out(1, 0)
    for k in range(4):
        for t in range(2):
            ring_up(t, k).wait_recv()
            if k < 3:
                ring_up(t, k + 1).start()
                if t == 0:
                    hand_out(0, k + 1)
                ring_down(t, k).wait_recv()
                if k < 2:
                    ring_down(t, k + 1).start()
                if t == 0:
                    hand_out(0, NY - 1 - k)
            elif t == 0:
                hand_out(0, 4)
        if k > 0:
            hand_out(1, k)
            hand_out(1, NY - k)
    hand_out(1, 4)

    none = jnp.zeros((BLK, HD), jnp.float32)
    for q in range(QB):
        terms_k[q, SEL] = none
        terms_v[q, SEL] = none
    for load in loads[3:]:
        load.wait()
    for q in range(QB):
        for h in range(GQA):
            gr[q : q + 1, h * BLK : (h + 1) * BLK] = gate_ref[h : h + 1, q * BLK : (q + 1) * BLK]
    gwp[...] = jnp.zeros_like(gwp)
    gw = gw_ref[...].astype(jnp.float32)
    for i in range(NZ):
        gwp[8 * i : 8 * i + GQA] = gw[GQA * i : GQA * (i + 1)]
    code_in.wait()
    pos_in.wait()

    def all_in(t):
        for r in range(NY):

            def landed(m, c, r=r):
                arrive(t, r, m).wait_recv()
                return c

            lax.fori_loop(1, NW, landed, 0)

    lanes = [slice(h * HD, (h + 1) * HD) for h in range(GQA)]
    below_diag = lax.broadcasted_iota(jnp.int32, (BLK, GQA * BLK), 0) - lax.rem(
        lax.broadcasted_iota(jnp.int32, (BLK, GQA * BLK), 1), BLK
    )

    def gather(t, q, p):
        at = code_s[p, lane + q]
        return tab[t][jnp.where(at < 0, NSEQ, at)]

    def gate_of(q):
        row = gr[pl.ds(q, 1), :]
        return row, jnp.broadcast_to(row, (HD, GQA * BLK))

    def score(q, c):
        rows = pl.ds(pl.multiple_of(q * BLK, BLK), BLK)
        qc = jnp.concatenate([q_ref[rows, a] for a in lanes], axis=0)
        gf = jnp.concatenate([g_ref[rows, a] for a in lanes], axis=0).astype(jnp.float32)
        da = (gate_of(q)[1].T * gf).astype(jnp.bfloat16)
        qc_ref[q] = qc
        da_ref[q] = da
        for p in range(SEL):
            kc[q, p * BLK : (p + 1) * BLK] = gather(0, q, p)
        st = dot(kc[q], qc, NT)
        parts = []
        for p in range(SEL):
            at = code_s[p, lane + q]
            reach = jnp.where(at == NSEQ + q, 0, jnp.where(at < 0, -BLK, BLK))
            parts.append(jnp.where(below_diag <= reach, st[p * BLK : (p + 1) * BLK], -jnp.inf))
        st = jnp.concatenate(parts, axis=0)
        top = jnp.max(st, axis=0, keepdims=True)
        e = jnp.exp2((st - top) * EXP2_SCALE)
        probs = e * (1.0 / jnp.sum(e, axis=0, keepdims=True))
        probs_ref[q] = probs
        terms_v[q, :SEL] = dot(probs.astype(jnp.bfloat16), da, NN).reshape(SEL, BLK, HD)
        return c

    def attend(q, c):
        rows = pl.ds(pl.multiple_of(q * BLK, BLK), BLK)
        for p in range(SEL):
            vc[p * BLK : (p + 1) * BLK] = gather(1, q, p)
        vals = vc[...]
        probs = probs_ref[q]
        qc = qc_ref[q]
        da = da_ref[q]
        att_t = dot(vals, probs.astype(jnp.bfloat16), TN)
        g_t = jnp.concatenate([g_ref[rows, a] for a in lanes], axis=0).astype(jnp.float32).T
        gate_row, gate_t = gate_of(q)
        da_t = (gate_t * g_t).astype(jnp.bfloat16).astype(jnp.float32)
        gsum = jnp.sum(g_t * att_t, axis=0, keepdims=True)
        ggrad = (gsum * gate_row * (1.0 - gate_row)).astype(jnp.bfloat16).astype(jnp.float32)
        gg[pl.ds(q, 1), :] = ggrad
        delta = jnp.sum(da_t * att_t, axis=0, keepdims=True)
        dp = dot(vals, da, NT)
        ds = (probs * (dp - delta)).astype(jnp.bfloat16)
        terms_k[q, :SEL] = (dot(ds, qc, NN) * SCALE).reshape(SEL, BLK, HD)
        dq = (dot(kc[q], ds, TN) * SCALE).T.astype(jnp.bfloat16)
        for h in range(GQA):
            dq_ref[rows, lanes[h]] = dq[h * BLK : (h + 1) * BLK]
        return c

    def give(t, r, m):
        return copy(snd.at[t, r, m], rx.at[t, r, m], y_s.at[t, r, m], y_r.at[t, r, m], mate(m))

    def summed(t, slot):
        total = terms[t][0, pos_s[slot, lane]]
        for q in range(1, QB):
            total = total + terms[t][q, pos_s[slot, lane + q]]
        return total

    def send_row(t, r):
        def one(i, c):
            m = lax.rem(i, NW)
            snd[t, r, m] = summed(t, row_of(r) * NW + lax.rem(w + m, NW)).astype(jnp.bfloat16)

            @pl.when(m > 0)
            def _():
                give(t, r, m).start()

            return c

        lax.fori_loop(1, NW + 1, one, 0)

    order = (4, 5, 3, 6, 2, 7, 1, 0)

    all_in(0)
    lax.fori_loop(0, QB, score, 0)
    for r in order:
        send_row(1, r)
    all_in(1)
    lax.fori_loop(0, QB, attend, 0)
    for r in order:
        send_row(0, r)
    dq_out = pltpu.make_async_copy(dq_ref, dq_hbm, out_s.at[0])
    dq_out.start()

    gbuf[z] = jnp.zeros((8, QB * BLK), jnp.float32)
    for q in range(QB):
        for h in range(GQA):
            gbuf[z, h : h + 1, q * BLK : (q + 1) * BLK] = gg[q : q + 1, h * BLK : (h + 1) * BLK]

    def gate_up(d):
        at = gbuf.at[lax.rem(z + NZ - max(d - 2, 0), NZ)]
        return copy(at, at, gu_s.at[d - 1], gu_r.at[d - 1], ahead[min(d, 2) - 1])

    def gate_up_in(d):
        at = gbuf.at[lax.rem(z + NZ - d, NZ)]
        return copy(at, at, gu_s.at[d - 1], gu_r.at[d - 1], ahead[min(d, 2) - 1])

    def gate_down(d):
        at = gbuf.at[lax.rem(z + max(d - 2, 0), NZ)]
        return copy(at, at, gd_s.at[d - 1], gd_r.at[d - 1], behind[min(d, 2) - 1])

    def gate_down_in(d):
        at = gbuf.at[lax.rem(z + d, NZ)]
        return copy(at, at, gd_s.at[d - 1], gd_r.at[d - 1], behind[min(d, 2) - 1])

    for d in (1, 2):
        gate_up(d).start()
        gate_down(d).start()

    def gate_step(k):
        for d in (2 * k - 1, 2 * k):
            gate_up_in(d).wait_recv()
            if d + 2 <= 8:
                gate_up(d + 2).start()
            if d <= 7:
                gate_down_in(d).wait_recv()
                if d + 2 <= 7:
                    gate_down(d + 2).start()

    def reduced(t, r):
        def wait(m, c):
            give(t, r, m).wait_recv()
            return c

        lax.fori_loop(1, NW, wait, 0)
        totals = [None] * QB
        for m in range(NW):
            val = (snd[t, r, 0] if m == 0 else rx[t, r, m]).astype(jnp.float32)
            which = asked(r, lax.rem(w + NW - m, NW))
            for j in range(QB):
                part = jnp.where(which == j, val, 0.0)
                totals[j] = part if m == 0 else totals[j] + part
        return totals

    def down(t, k):
        return copy(dn_out.at[t, k], dn_in.at[t, k - 1], dn_s.at[t, k], dn_r.at[t, k], below)

    def up(t, k):
        return copy(up_out.at[t, k], up_in.at[t, k - 1], up_s.at[t, k], up_r.at[t, k], above)

    def pass_on(t, r):
        totals = reduced(t, r)
        if r <= 4:
            k, inn, out, hop, last = r, dn_in, dn_out, down, 4
        else:
            k, inn, out, hop, last = NY - r, up_in, up_out, up, 3
        if k < last:
            hop(t, k + 1).wait_recv()
        for j in range(QB):
            val = totals[j]
            if k < last:
                val = val + inn[t, k, j].astype(jnp.float32)
            out[t, k, j] = val.astype(jnp.bfloat16)
        hop(t, k).start()

    def finish(t, ref):
        totals = reduced(t, 0)
        down(t, 1).wait_recv()
        up(t, 1).wait_recv()
        for j in range(QB):
            val = totals[j] + summed(t, NSEQ + j)
            val = val + dn_in[t, 0, j].astype(jnp.float32) + up_in[t, 0, j].astype(jnp.float32)
            ref[j] = val.astype(jnp.bfloat16)

    pass_on(1, 4)
    pass_on(1, 5)
    pass_on(1, 3)
    gate_step(1)
    pass_on(1, 6)
    pass_on(0, 4)
    pass_on(0, 5)
    pass_on(1, 2)
    gate_step(2)
    pass_on(1, 7)
    pass_on(0, 3)
    pass_on(0, 6)
    pass_on(1, 1)
    gate_step(3)
    pass_on(0, 2)
    pass_on(0, 7)
    finish(1, dv_ref)
    gate_step(4)
    pass_on(0, 1)
    gates = gbuf[...].reshape(NZ * 8, QB * BLK).astype(jnp.bfloat16)
    gi_ref[...] = dot(gwp[...].astype(jnp.bfloat16), gates, TN).astype(jnp.bfloat16)
    gi_out = pltpu.make_async_copy(gi_ref, gi_hbm, out_s.at[1])
    gi_out.start()
    finish(0, dk_ref)

    for t in range(2):
        for k in range(4):
            ring_up(t, k).wait_send()
            down(t, k + 1).wait_send()
        for k in range(3):
            ring_down(t, k).wait_send()
            up(t, k + 1).wait_send()
        for r in range(NY):

            def sent(m, c, t=t, r=r):
                fetch(t, r, m).wait_send()
                give(t, r, m).wait_send()
                return c

            lax.fori_loop(1, NW, sent, 0)
    for d in range(1, 9):
        gate_up(d).wait_send()
        if d < 8:
            gate_down(d).wait_send()
    dq_out.wait()
    gi_out.wait()


def place(*refs):
    half = len(refs) // 2
    for src, dst in zip(refs[:half], refs[half:]):
        dst[...] = src[...]


def shards(queries, keys, values, grad_out, gate, gate_weight, selection):
    vmem = pl.BlockSpec(memory_space=pltpu.VMEM)
    hbm = pl.BlockSpec(memory_space=pl.ANY)
    bf, f32, i32 = jnp.bfloat16, jnp.float32, jnp.int32
    dma = pltpu.SemaphoreType.DMA
    blocks = (QB, BLK, HD)
    tokens, width = queries.shape
    depth = gate_weight.shape[1]
    outs = (
        jax.ShapeDtypeStruct(queries.shape, bf),
        jax.ShapeDtypeStruct(blocks, bf),
        jax.ShapeDtypeStruct(blocks, bf),
        jax.ShapeDtypeStruct((depth, tokens), bf),
    )
    results = pl.pallas_call(
        kernel,
        out_shape=outs,
        in_specs=[hbm] * 7,
        out_specs=(hbm, vmem, vmem, hbm),
        scratch_shapes=[pltpu.VMEM(blocks, bf) for _ in range(2 * NY)]
        + [
            pltpu.VMEM((tokens, width), bf),
            pltpu.VMEM((tokens, width), bf),
            pltpu.VMEM((GQA, tokens), f32),
            pltpu.VMEM((NZ * GQA, depth), bf),
            pltpu.VMEM((SEL, NSEQ * QB), i32),
            pltpu.VMEM((tokens, width), bf),
            pltpu.VMEM((depth, tokens), bf),
            pltpu.VMEM((NY + SEL + NSEQ + 8, NSEQ * QB), i32),
            pltpu.SMEM((NY, HD), i32),
            pltpu.SMEM((SEL, HD), i32),
            pltpu.SMEM((NSEQ + 8, HD), i32),
            pltpu.VMEM((2, NY, NW, BLK, HD), bf),
            pltpu.VMEM((NSEQ + QB, BLK, HD), bf),
            pltpu.VMEM((NSEQ + QB, BLK, HD), bf),
            pltpu.VMEM((QB, SEL * BLK, HD), bf),
            pltpu.VMEM((SEL * BLK, HD), bf),
            pltpu.VMEM((QB, SEL * BLK, GQA * BLK), f32),
            pltpu.VMEM((QB, GQA * BLK, HD), bf),
            pltpu.VMEM((QB, GQA * BLK, HD), bf),
            pltpu.VMEM((QB, SEL + 1, BLK, HD), f32),
            pltpu.VMEM((QB, SEL + 1, BLK, HD), f32),
            pltpu.VMEM((8, GQA * BLK), f32),
            pltpu.VMEM((8, GQA * BLK), f32),
            pltpu.VMEM((NZ, 8, QB * BLK), f32),
            pltpu.VMEM((NZ * 8, depth), f32),
            pltpu.VMEM((2, NY, NW, BLK, HD), bf),
            pltpu.VMEM((2, NY, NW, BLK, HD), bf),
            pltpu.VMEM((2, 5) + blocks, bf),
            pltpu.VMEM((2, 4) + blocks, bf),
            pltpu.VMEM((2, 4) + blocks, bf),
            pltpu.VMEM((2, 3) + blocks, bf),
            dma((9,)), dma((2,)), dma((3,)),
            dma((2, 4)), dma((2, 4)), dma((2, 3)), dma((2, 3)),
            dma((2, NY, NW)), dma((2, NY, NW)), dma((2, NY, NW)), dma((2, NY, NW)),
            dma((2, 5)), dma((2, 5)), dma((2, 4)), dma((2, 4)),
            dma((8,)), dma((8,)), dma((7,)), dma((7,)),
        ],
        compiler_params=pltpu.CompilerParams(
            collective_id=0, has_side_effects=True, vmem_limit_bytes=56 << 20
        ),
    )(
        queries,
        keys.reshape(blocks),
        values.reshape(blocks),
        grad_out,
        gate.T,
        gate_weight,
        selection.transpose(1, 2, 0)[0],
    )
    dq, dk, dv, gi = pl.pallas_call(
        place,
        out_shape=outs,
        in_specs=[vmem] * 4,
        out_specs=(vmem,) * 4,
        compiler_params=pltpu.CompilerParams(vmem_limit_bytes=56 << 20),
    )(*results)
    return dq, dk.reshape(keys.shape), dv.reshape(values.shape), gi.T


def solution(mesh):
    placed = (
        P("seq", "head"),
        P("seq", "head"),
        P("seq", "head"),
        P("seq", "head"),
        P("seq", "head"),
        P(None, "head"),
        P(None, "head", None),
    )
    return jax.shard_map(
        shards,
        mesh=mesh,
        in_specs=placed,
        out_specs=(P("seq", "head"), P("seq", "head"), P("seq", "head"), P("seq", "head")),
        check_vma=False,
    )
```

time: 248 us -> 86.3 us (0.35)
  Pallas kernels: 0 us -> 85.3 us
  waiting for transfers between devices: 84 us -> 0 us
  blocking collectives: 81.8 us -> 0 us
  matrix products: 28.8 us -> 0 us
  local copies, waits for them, and re-layouts: 25.9 us -> 0 us
  starting transfers between devices: 17.3 us -> 0 us
  other arithmetic: 7.64 us -> 0 us
    pallas_call x0 -> x2, Pallas kernels: none -> 85.3 us  [the longest x1 83.3 us: shards(): pl.pallas_call(kernel, out_shape=outs, in_specs=[hbm] * 7, out_specs=(hbm...]
    all_to_all x3 -> x0, waiting for transfers between devices: 84 us -> none  [the longest x1 49.3 us: shards(): lax.all_to_all(key_acc[qb_dev:], 'seq', split_axis=0, concat_axis=0, tile...]
    all_to_all x1 -> x0, blocking collectives: 46.1 us -> none  [shards(): lax.all_to_all(outgoing[0], 'seq', split_axis=0, concat_axis=0, tiled=True)]
    all_gather x1 -> x0, blocking collectives: 35.7 us -> none  [shards(): lax.all_gather(gate_local, 'head', axis=1, tiled=True)]
    dot_general x19 -> x0, matrix products: 28.8 us -> none  [the longest x4 11.7 us: scatter_rows(): jnp.einsum('nsr,nskh->rkh', onehot, blocked, precision=lax.Precision.HIGH...]
    all_to_all x3 -> x0, starting transfers between devices: 17.3 us -> none  [the longest x1 5.84 us: shards(): lax.all_to_all(outgoing[1], 'seq', split_axis=0, concat_axis=0, tiled=True)]
    gather x6 -> x0, local copies, waits for them, and re-layouts: 9.92 us -> none  [the longest x2 3.79 us: forward_part(): key_flat = key_table[rows_tile].reshape(2, picks_len * BLK, head_dim)]
    while x50 -> x0, local copies, waits for them, and re-layouts: 5.45 us -> none
  transfers between devices with their start and end apart: 3 -> 0, of which waited for: 3 -> 0; matrix products, arithmetic and copies ran while one was open for 5% -> 0% of each run, Pallas kernels for 0% -> 0%
where the time goes in v2:
time: 86.3 us; the launch traced here: 85.9 us
  Pallas kernels  85.3 us (99%)
    pallas_call x1, Pallas kernels, shards(): pl.pallas_call(kernel, out_shape=outs, in_specs=[hbm] * 7, out_specs=(hbm...  83.3 us
    pallas_call x1, Pallas kernels, shards(): pl.pallas_call(place, out_shape=outs, in_specs=[vmem] * 4, out_specs=(vme...  1.91 us

profile of v2, /device:TPU:6, one launch (start us, length us, event | category | flops | bytes accessed | tf_op | source)
XLA Modules:
  0.0 85.9 jit_solution(17680954833261374249)
XLA Ops:
  0.6 83.3 %shard_map.102 = (bf16[256,512]{1,0:T(8,128)(2,1)}, bf16[4,64,128]{2,1,0:T(8,128)(2,1)}, bf16[4,64,128]{2,1,0:T(8,128)(2,1)}, bf16[448,256]{1,0:T(8,128)(2,1)}) custom-call(bf16[256,512]{1,0:T(8,128)(2,1)} %q_hbm.1, bf16[4,64,128]{2,1,0:T(8,128)(2,1)} %bitcast.9, bf16[4,64,128]{2,1,0:T(8,128)(2,1)} %bitcast.10, bf16[256,512]{1,0:T(8,128)(2,1)} %g_hbm.1, ...), custom_call_target="tpu_custom_call" | custom-call | tf_op jit(solution)/shard_map/pallas_call | solution.py:443
  84.0 1.9 %shard_map.103 = (bf16[256,512]{1,0:T(8,128)(2,1)}, bf16[4,64,128]{2,1,0:T(8,128)(2,1)}, bf16[4,64,128]{2,1,0:T(8,128)(2,1)}, bf16[448,256]{1,0:T(8,128)(2,1)}) custom-call(bf16[256,512]{1,0:T(8,128)(2,1)} %get-tuple-element.12.refs_0_, bf16[4,64,128]{2,1,0:T(8,128)(2,1)} %get-tuple-element.13.refs_1_, bf16[4,64,128]{2,1,0:T(8,128)(2,1)} %get-tuple-element.14.refs_2_, ...), custom_call_target="tpu_custom_call" | custom-call | tf_op jit(solution)/shard_map/pallas_call | solution.py:499

commit v3 on v2

--- a/solution.py
+++ b/solution.py
@@ -17,6 +17,8 @@
 NW = 8
 NZ = 16
 NSEQ = NY * NW
+REACH = 6
+CUTS = 4
 MESH = pl.DeviceIdType.MESH
 SCALE = 1.0 / math.sqrt(HD)
 EXP2_SCALE = SCALE / math.log(2.0)
@@ -36,14 +38,16 @@
     dq_hbm, dk_ref, dv_ref, gi_hbm,
     *scratch,
 ):
-    cols = (scratch[:NY], scratch[NY : 2 * NY])
+    cols = (scratch[:REACH], scratch[REACH : 2 * REACH])
     (
         q_ref, g_ref, gate_ref, gw_ref, sel_ref, dq_ref, gi_ref,
-        tbl, req_s, code_s, pos_s,
+        ds_ref, tbl, req_s, code_s, pos_s,
         stage, tab_k, tab_v, kc, vc, probs_ref, qc_ref, da_ref, terms_k, terms_v,
-        gr, gg, gbuf, gwp, snd, rx, dn_out, dn_in, up_out, up_in,
-        in_s, out_s, t_s, f_s, f_r, b_s, b_r, x_s, x_r, y_s, y_r, dn_s, dn_r, up_s, up_r, gu_s, gu_r, gd_s, gd_r,
-    ) = scratch[2 * NY :]
+        gr, gg, gbuf, gwp, snd, rx, sum_out, sum_in, fin,
+        far_stage, far_tab, far_snd, far_rx, far_in,
+        in_s, out_s, t_s, f_s, f_r, x_s, x_r, y_s, y_r, d_s, d_r, gu_s, gu_r, gd_s, gd_r,
+        fx_s, fx_r, fy_s, fy_r, by_s, by_r, bx_s, bx_r,
+    ) = scratch[2 * REACH :]
     tab = (tab_k, tab_v)
     terms = (terms_k, terms_v)
     s = lax.axis_index("seq")
@@ -57,15 +61,16 @@
     def row_of(r):
         return lax.rem(y + (NY - r), NY)
 
-    above = (lax.rem(y + 1, NY) * NW + w, z)
-    below = (lax.rem(y + NY - 1, NY) * NW + w, z)
+    def up_by(n):
+        return (lax.rem(y + n + NY, NY) * NW + w, z)
+
     ahead = [(s, lax.rem(z + i, NZ)) for i in (1, 2)]
     behind = [(s, lax.rem(z + NZ - i, NZ)) for i in (1, 2)]
 
     barrier = pltpu.get_barrier_semaphore()
     for m in range(1, NW):
         pl.semaphore_signal(barrier, inc=1, device_id=mate(m), device_id_type=MESH)
-    for to in (above, below, *ahead, *behind):
+    for to in (up_by(1), up_by(-1), up_by(2), up_by(-2), *ahead, *behind):
         pl.semaphore_signal(barrier, inc=1, device_id=to, device_id_type=MESH)
 
     loads = [
@@ -93,7 +98,7 @@
         req = jnp.where(owner[p : p + 1] == mine, inner[p : p + 1], req)
     tbl[0:NY] = req
     half = pl.ds(pl.multiple_of(y // 4 * HD, HD), HD)
-    req_in = pltpu.make_async_copy(tbl.at[pl.ds(0, NY), half], req_s, t_s.at[0])
+    req_in = pltpu.make_async_copy(tbl.at[pl.ds(0, NY)], req_s, t_s.at[0])
     req_in.start()
     pos = jnp.full((NSEQ + 8, NSEQ * QB), SEL, jnp.int32)
     for p in range(SEL):
@@ -104,30 +109,38 @@
     pos_in = pltpu.make_async_copy(tbl.at[pl.ds(NY + SEL, NSEQ + 8), half], pos_s, t_s.at[2])
     code_in.start()
     pos_in.start()
-    row_lane = lax.rem(y, 4) * (NW * QB)
-    lane = row_lane + w * QB
-
-    def asked(r, d):
-        at = row_lane + d * QB
-        got = req_s[row_of(r), at]
+    lane = lax.rem(s * QB, HD)
+
+    def asked(row, d):
+        got = req_s[row, d * QB]
         for q in range(1, QB):
-            got = jnp.maximum(got, req_s[row_of(r), at + q])
+            got = jnp.maximum(got, req_s[row, d * QB + q])
         return got
 
     loads[0].wait()
     loads[1].wait()
-    pl.semaphore_wait(barrier, NW + 5)
+    pl.semaphore_wait(barrier, NW + 7)
 
     def copy(src, dst, send, recv, to):
         return pltpu.make_async_remote_copy(
             src_ref=src, dst_ref=dst, send_sem=send, recv_sem=recv, device_id=to, device_id_type=MESH
         )
 
-    def ring_up(t, k):
-        return copy(cols[t][k], cols[t][k + 1], f_s.at[t, k], f_r.at[t, k], above)
-
-    def ring_down(t, k):
-        return copy(cols[t][(NY - k) % NY], cols[t][NY - 1 - k], b_s.at[t, k], b_r.at[t, k], below)
+    def spread(t, r, c):
+        part = pl.ds(c * (QB // CUTS), QB // CUTS)
+        return copy(
+            cols[t][r - 1].at[part], cols[t][r].at[part], f_s.at[t, r, c], f_r.at[t, r, c], up_by(1)
+        )
+
+    def spread_start(t, r, c):
+        @pl.when((y >= r - 1) & (y < NY - 1))
+        def _():
+            spread(t, r, c).start()
+
+    def spread_in(t, r, c):
+        @pl.when(y >= r)
+        def _():
+            spread(t, r, c).wait_recv()
 
     def fetch(t, r, m):
         return copy(stage.at[t, r, m], tab[t].at[row_of(r) * NW + w], x_s.at[t, r, m], x_r.at[t, r, m], mate(m))
@@ -137,40 +150,86 @@
         return copy(stage.at[t, r, m], tab[t].at[home], x_s.at[t, r, m], x_r.at[t, r, m], mate(m))
 
     def hand_out(t, r):
-        tab[t][row_of(r) * NW + w] = cols[t][r][jnp.maximum(asked(r, w), 0)]
-
-        def one(m, c):
-            block = jnp.maximum(asked(r, lax.rem(w + m, NW)), 0)
-            stage[t, r, m] = cols[t][r][block]
-            fetch(t, r, m).start()
-            return c
-
-        lax.fori_loop(1, NW, one, 0)
-
+        @pl.when(y >= r)
+        def _():
+            row = row_of(r)
+            tab[t][row * NW + w] = cols[t][r][jnp.maximum(asked(row, s), 0)]
+
+            def one(m, c):
+                block = jnp.maximum(asked(row, y * NW + lax.rem(w + m, NW)), 0)
+                stage[t, r, m] = cols[t][r][block]
+                fetch(t, r, m).start()
+                return c
+
+            lax.fori_loop(1, NW, one, 0)
+
+    def far_row(j):
+        return NY - 1 - j
+
+    def far_fetch(t, j, m):
+        return copy(far_stage.at[t, j, m], far_tab.at[t, j, w], fx_s.at[t, j, m], fx_r.at[t, j, m], mate(m))
+
+    def far_arrive(t, j, m):
+        at = lax.rem(w + NW - m, NW)
+        return copy(far_stage.at[t, j, m], far_tab.at[t, j, at], fx_s.at[t, j, m], fx_r.at[t, j, m], mate(m))
+
+    def far_push(t, j):
+        return copy(
+            far_tab.at[t, j], tab[t].at[pl.ds(y * NW, NW)], fy_s.at[t, j], fy_r.at[t, y], (far_row(j) * NW + w, z)
+        )
+
+    def far_landed(t, o):
+        return copy(far_tab.at[t, 0], tab[t].at[pl.ds(o * NW, NW)], fy_s.at[t, 0], fy_r.at[t, o], up_by(1))
+
+    def far_hand_out(t):
+        for j in range(2):
+
+            @pl.when(y < 2 - j)
+            def _(j=j):
+                far_tab[t, j, w] = cols[t][0][jnp.maximum(asked(y, far_row(j) * NW + w), 0)]
+
+                def one(m, c):
+                    block = jnp.maximum(asked(y, far_row(j) * NW + lax.rem(w + m, NW)), 0)
+                    far_stage[t, j, m] = cols[t][0][block]
+                    far_fetch(t, j, m).start()
+                    return c
+
+                lax.fori_loop(1, NW, one, 0)
+
+    def far_forward(t):
+        for j in range(2):
+
+            @pl.when(y < 2 - j)
+            def _(j=j):
+                def landed(m, c):
+                    far_arrive(t, j, m).wait_recv()
+                    return c
+
+                lax.fori_loop(1, NW, landed, 0)
+                far_push(t, j).start()
+
+    for c in range(CUTS):
+        for t in range(2):
+            spread_start(t, 1, c)
+    req_in.wait()
     for t in range(2):
-        ring_up(t, 0).start()
-        ring_down(t, 0).start()
-    req_in.wait()
-    hand_out(0, 0)
-    hand_out(1, 0)
-    for k in range(4):
-        for t in range(2):
-            ring_up(t, k).wait_recv()
-            if k < 3:
-                ring_up(t, k + 1).start()
-                if t == 0:
-                    hand_out(0, k + 1)
-                ring_down(t, k).wait_recv()
-                if k < 2:
-                    ring_down(t, k + 1).start()
-                if t == 0:
-                    hand_out(0, NY - 1 - k)
-            elif t == 0:
-                hand_out(0, 4)
-        if k > 0:
-            hand_out(1, k)
-            hand_out(1, NY - k)
-    hand_out(1, 4)
+        hand_out(t, 0)
+        far_hand_out(t)
+    for k in range(1, REACH + 1):
+        if k < REACH:
+            for c in range(CUTS):
+                spread_in(0, k, c)
+                if k < REACH - 1:
+                    spread_start(0, k + 1, c)
+            hand_out(0, k)
+        if k > 1:
+            for c in range(CUTS):
+                spread_in(1, k - 1, c)
+                if k < REACH:
+                    spread_start(1, k, c)
+            hand_out(1, k - 1)
+        if k < 3:
+            far_forward(k - 1)
 
     none = jnp.zeros((BLK, HD), jnp.float32)
     for q in range(QB):
@@ -189,13 +248,21 @@
     pos_in.wait()
 
     def all_in(t):
-        for r in range(NY):
-
-            def landed(m, c, r=r):
-                arrive(t, r, m).wait_recv()
-                return c
-
-            lax.fori_loop(1, NW, landed, 0)
+        for r in range(REACH):
+
+            @pl.when(y >= r)
+            def _(r=r):
+                def landed(m, c):
+                    arrive(t, r, m).wait_recv()
+                    return c
+
+                lax.fori_loop(1, NW, landed, 0)
+
+        for o in range(2):
+
+            @pl.when(y >= NY - 2 + o)
+            def _(o=o):
+                far_landed(t, o).wait_recv()
 
     lanes = [slice(h * HD, (h + 1) * HD) for h in range(GQA)]
     below_diag = lax.broadcasted_iota(jnp.int32, (BLK, GQA * BLK), 0) - lax.rem(
@@ -252,10 +319,14 @@
         dp = dot(vals, da, NT)
         ds = (probs * (dp - delta)).astype(jnp.bfloat16)
         terms_k[q, :SEL] = (dot(ds, qc, NN) * SCALE).reshape(SEL, BLK, HD)
-        dq = (dot(kc[q], ds, TN) * SCALE).T.astype(jnp.bfloat16)
+        ds_ref[q] = ds
+        return c
+
+    def query(q):
+        rows = slice(q * BLK, (q + 1) * BLK)
+        dq = (dot(kc[q], ds_ref[q], TN) * SCALE).T.astype(jnp.bfloat16)
         for h in range(GQA):
             dq_ref[rows, lanes[h]] = dq[h * BLK : (h + 1) * BLK]
-        return c
 
     def give(t, r, m):
         return copy(snd.at[t, r, m], rx.at[t, r, m], y_s.at[t, r, m], y_r.at[t, r, m], mate(m))
@@ -267,30 +338,150 @@
         return total
 
     def send_row(t, r):
-        def one(i, c):
-            m = lax.rem(i, NW)
-            snd[t, r, m] = summed(t, row_of(r) * NW + lax.rem(w + m, NW)).astype(jnp.bfloat16)
-
-            @pl.when(m > 0)
-            def _():
-                give(t, r, m).start()
-
+        @pl.when(y >= r)
+        def _():
+            def one(i, c):
+                m = lax.rem(i, NW)
+                snd[t, r, m] = summed(t, row_of(r) * NW + lax.rem(w + m, NW)).astype(jnp.bfloat16)
+
+                @pl.when(m > 0)
+                def _():
+                    give(t, r, m).start()
+
+                return c
+
+            lax.fori_loop(1, NW + 1, one, 0)
+
+    def far_give(t, o):
+        to = (o * NW + w, z)
+        return copy(far_snd.at[t, o], far_rx.at[t, NY - 1 - y], by_s.at[t, o], by_r.at[t, NY - 1 - y], to)
+
+    def far_given(t, j):
+        return copy(far_snd.at[t, 0], far_rx.at[t, j], by_s.at[t, 0], by_r.at[t, j], up_by(1))
+
+    def far_send(t):
+        for o in range(2):
+
+            @pl.when(y >= NY - 2 + o)
+            def _(o=o):
+                def one(i, c):
+                    far_snd[t, o, i] = summed(t, o * NW + i).astype(jnp.bfloat16)
+                    return c
+
+                lax.fori_loop(0, NW, one, 0)
+                far_give(t, o).start()
+
+    def far_deal(t, j, m):
+        return copy(
+            far_rx.at[t, j, lax.rem(w + m, NW)], far_in.at[t, j, m], bx_s.at[t, j, m], bx_r.at[t, j, m], mate(m)
+        )
+
+    def far_relay(t):
+        for j in range(2):
+
+            @pl.when(y < 2 - j)
+            def _(j=j):
+                far_given(t, j).wait_recv()
+
+                def one(m, c):
+                    far_deal(t, j, m).start()
+                    return c
+
+                lax.fori_loop(1, NW, one, 0)
+
+    def sorted_sum(vals, row, devs):
+        totals = [None] * QB
+        for m in range(NW):
+            val = vals(m).astype(jnp.float32)
+            which = asked(row, devs(m))
+            for j in range(QB):
+                part = jnp.where(which == j, val, 0.0)
+                totals[j] = part if m == 0 else totals[j] + part
+        return totals
+
+    def reduced(t, r):
+        def wait(m, c):
+            give(t, r, m).wait_recv()
             return c
 
-        lax.fori_loop(1, NW + 1, one, 0)
-
-    order = (4, 5, 3, 6, 2, 7, 1, 0)
+        lax.fori_loop(1, NW, wait, 0)
+        return sorted_sum(
+            lambda m: snd[t, r, 0] if m == 0 else rx[t, r, m],
+            row_of(r),
+            lambda m: y * NW + lax.rem(w + NW - m, NW),
+        )
+
+    def hop(t, r, j):
+        return copy(sum_out.at[t, r, j], sum_in.at[t, r, j], d_s.at[t, r, j], d_r.at[t, r, j], up_by(-1))
+
+    def hop_in(t, r, j):
+        @pl.when(y < NY - 1)
+        def _():
+            hop(t, r, j).wait_recv()
+
+    def no_hop_in(t, r):
+        @pl.when(y >= NY - 1)
+        def _():
+            sum_in[t, r] = jnp.zeros((QB, BLK, HD), jnp.bfloat16)
+
+    def pass_on(t, r):
+        @pl.when(y >= r)
+        def _():
+            totals = reduced(t, r)
+            if r < REACH - 1:
+                no_hop_in(t, r + 1)
+            for j in range(QB):
+                val = totals[j]
+                if r < REACH - 1:
+                    hop_in(t, r + 1, j)
+                    val = val + sum_in[t, r + 1, j].astype(jnp.float32)
+                sum_out[t, r, j] = val.astype(jnp.bfloat16)
+                hop(t, r, j).start()
+
+    def finish(t, ref):
+        totals = reduced(t, 0)
+        for j in range(QB):
+            fin[j] = totals[j] + summed(t, NSEQ + j)
+        for i in range(2):
+
+            @pl.when(y < 2 - i)
+            def _(i=i):
+                def wait(m, c):
+                    far_deal(t, i, m).wait_recv()
+                    return c
+
+                lax.fori_loop(1, NW, wait, 0)
+                more = sorted_sum(
+                    lambda m: far_rx[t, i, w] if m == 0 else far_in[t, i, m],
+                    y,
+                    lambda m: far_row(i) * NW + lax.rem(w + NW - m, NW),
+                )
+                for j in range(QB):
+                    fin[j] += more[j]
+
+        no_hop_in(t, 1)
+        for j in range(QB):
+            hop_in(t, 1, j)
+            val = fin[j] + sum_in[t, 1, j].astype(jnp.float32)
+            ref[j] = val.astype(jnp.bfloat16)
+
+    order = (5, 4, 3, 2, 1, 0)
 
     all_in(0)
     lax.fori_loop(0, QB, score, 0)
-    for r in order:
+    send_row(1, 5)
+    far_send(1)
+    for r in order[1:]:
         send_row(1, r)
     all_in(1)
-    lax.fori_loop(0, QB, attend, 0)
-    for r in order:
+    lax.fori_loop(0, QB // 2, attend, 0)
+    pass_on(1, 5)
+    lax.fori_loop(QB // 2, QB, attend, 0)
+    send_row(0, 5)
+    send_row(0, 4)
+    far_send(0)
+    for r in order[2:]:
         send_row(0, r)
-    dq_out = pltpu.make_async_copy(dq_ref, dq_hbm, out_s.at[0])
-    dq_out.start()
 
     gbuf[z] = jnp.zeros((8, QB * BLK), jnp.float32)
     for q in range(QB):
@@ -327,70 +518,28 @@
                 if d + 2 <= 7:
                     gate_down(d + 2).start()
 
-    def reduced(t, r):
-        def wait(m, c):
-            give(t, r, m).wait_recv()
-            return c
-
-        lax.fori_loop(1, NW, wait, 0)
-        totals = [None] * QB
-        for m in range(NW):
-            val = (snd[t, r, 0] if m == 0 else rx[t, r, m]).astype(jnp.float32)
-            which = asked(r, lax.rem(w + NW - m, NW))
-            for j in range(QB):
-                part = jnp.where(which == j, val, 0.0)
-                totals[j] = part if m == 0 else totals[j] + part
-        return totals
-
-    def down(t, k):
-        return copy(dn_out.at[t, k], dn_in.at[t, k - 1], dn_s.at[t, k], dn_r.at[t, k], below)
-
-    def up(t, k):
-        return copy(up_out.at[t, k], up_in.at[t, k - 1], up_s.at[t, k], up_r.at[t, k], above)
-
-    def pass_on(t, r):
-        totals = reduced(t, r)
-        if r <= 4:
-            k, inn, out, hop, last = r, dn_in, dn_out, down, 4
-        else:
-            k, inn, out, hop, last = NY - r, up_in, up_out, up, 3
-        if k < last:
-            hop(t, k + 1).wait_recv()
-        for j in range(QB):
-            val = totals[j]
-            if k < last:
-                val = val + inn[t, k, j].astype(jnp.float32)
-            out[t, k, j] = val.astype(jnp.bfloat16)
-        hop(t, k).start()
-
-    def finish(t, ref):
-        totals = reduced(t, 0)
-        down(t, 1).wait_recv()
-        up(t, 1).wait_recv()
-        for j in range(QB):
-            val = totals[j] + summed(t, NSEQ + j)
-            val = val + dn_in[t, 0, j].astype(jnp.float32) + up_in[t, 0, j].astype(jnp.float32)
-            ref[j] = val.astype(jnp.bfloat16)
-
     pass_on(1, 4)
-    pass_on(1, 5)
+    far_relay(1)
+    pass_on(0, 5)
+    query(0)
     pass_on(1, 3)
     gate_step(1)
-    pass_on(1, 6)
     pass_on(0, 4)
-    pass_on(0, 5)
+    query(1)
     pass_on(1, 2)
     gate_step(2)
-    pass_on(1, 7)
     pass_on(0, 3)
-    pass_on(0, 6)
+    query(2)
+    far_relay(0)
     pass_on(1, 1)
+    pass_on(0, 2)
+    query(3)
+    dq_out = pltpu.make_async_copy(dq_ref, dq_hbm, out_s.at[0])
+    dq_out.start()
     gate_step(3)
-    pass_on(0, 2)
-    pass_on(0, 7)
     finish(1, dv_ref)
+    pass_on(0, 1)
     gate_step(4)
-    pass_on(0, 1)
     gates = gbuf[...].reshape(NZ * 8, QB * BLK).astype(jnp.bfloat16)
     gi_ref[...] = dot(gwp[...].astype(jnp.bfloat16), gates, TN).astype(jnp.bfloat16)
     gi_out = pltpu.make_async_copy(gi_ref, gi_hbm, out_s.at[1])
@@ -398,20 +547,45 @@
     finish(0, dk_ref)
 
     for t in range(2):
-        for k in range(4):
-            ring_up(t, k).wait_send()
-            down(t, k + 1).wait_send()
-        for k in range(3):
-            ring_down(t, k).wait_send()
-            up(t, k + 1).wait_send()
-        for r in range(NY):
-
-            def sent(m, c, t=t, r=r):
-                fetch(t, r, m).wait_send()
-                give(t, r, m).wait_send()
-                return c
-
-            lax.fori_loop(1, NW, sent, 0)
+        for r in range(1, REACH):
+
+            @pl.when((y >= r - 1) & (y < NY - 1))
+            def _(t=t, r=r):
+                for c in range(CUTS):
+                    spread(t, r, c).wait_send()
+
+            @pl.when(y >= r)
+            def _(t=t, r=r):
+                for j in range(QB):
+                    hop(t, r, j).wait_send()
+
+        for r in range(REACH):
+
+            @pl.when(y >= r)
+            def _(t=t, r=r):
+                def sent(m, c):
+                    fetch(t, r, m).wait_send()
+                    give(t, r, m).wait_send()
+                    return c
+
+                lax.fori_loop(1, NW, sent, 0)
+
+        for j in range(2):
+
+            @pl.when(y < 2 - j)
+            def _(t=t, j=j):
+                def sent(m, c):
+                    far_fetch(t, j, m).wait_send()
+                    far_deal(t, j, m).wait_send()
+                    return c
+
+                lax.fori_loop(1, NW, sent, 0)
+                far_push(t, j).wait_send()
+
+            @pl.when(y >= NY - 2 + j)
+            def _(t=t, j=j):
+                far_give(t, j).wait_send()
+
     for d in range(1, 9):
         gate_up(d).wait_send()
         if d < 8:
@@ -445,7 +619,7 @@
         out_shape=outs,
         in_specs=[hbm] * 7,
         out_specs=(hbm, vmem, vmem, hbm),
-        scratch_shapes=[pltpu.VMEM(blocks, bf) for _ in range(2 * NY)]
+        scratch_shapes=[pltpu.VMEM(blocks, bf) for _ in range(2 * REACH)]
         + [
             pltpu.VMEM((tokens, width), bf),
             pltpu.VMEM((tokens, width), bf),
@@ -454,11 +628,12 @@
             pltpu.VMEM((SEL, NSEQ * QB), i32),
             pltpu.VMEM((tokens, width), bf),
             pltpu.VMEM((depth, tokens), bf),
+            pltpu.VMEM((QB, SEL * BLK, GQA * BLK), bf),
             pltpu.VMEM((NY + SEL + NSEQ + 8, NSEQ * QB), i32),
-            pltpu.SMEM((NY, HD), i32),
+            pltpu.SMEM((NY, NSEQ * QB), i32),
             pltpu.SMEM((SEL, HD), i32),
             pltpu.SMEM((NSEQ + 8, HD), i32),
-            pltpu.VMEM((2, NY, NW, BLK, HD), bf),
+            pltpu.VMEM((2, REACH, NW, BLK, HD), bf),
             pltpu.VMEM((NSEQ + QB, BLK, HD), bf),
             pltpu.VMEM((NSEQ + QB, BLK, HD), bf),
             pltpu.VMEM((QB, SEL * BLK, HD), bf),
@@ -472,17 +647,23 @@
             pltpu.VMEM((8, GQA * BLK), f32),
             pltpu.VMEM((NZ, 8, QB * BLK), f32),
             pltpu.VMEM((NZ * 8, depth), f32),
-            pltpu.VMEM((2, NY, NW, BLK, HD), bf),
-            pltpu.VMEM((2, NY, NW, BLK, HD), bf),
-            pltpu.VMEM((2, 5) + blocks, bf),
-            pltpu.VMEM((2, 4) + blocks, bf),
-            pltpu.VMEM((2, 4) + blocks, bf),
-            pltpu.VMEM((2, 3) + blocks, bf),
+            pltpu.VMEM((2, REACH, NW, BLK, HD), bf),
+            pltpu.VMEM((2, REACH, NW, BLK, HD), bf),
+            pltpu.VMEM((2, REACH) + blocks, bf),
+            pltpu.VMEM((2, REACH) + blocks, bf),
+            pltpu.VMEM(blocks, f32),
+            pltpu.VMEM((2, 2, NW, BLK, HD), bf),
+            pltpu.VMEM((2, 2, NW, BLK, HD), bf),
+            pltpu.VMEM((2, 2, NW, BLK, HD), bf),
+            pltpu.VMEM((2, 2, NW, BLK, HD), bf),
+            pltpu.VMEM((2, 2, NW, BLK, HD), bf),
             dma((9,)), dma((2,)), dma((3,)),
-            dma((2, 4)), dma((2, 4)), dma((2, 3)), dma((2, 3)),
-            dma((2, NY, NW)), dma((2, NY, NW)), dma((2, NY, NW)), dma((2, NY, NW)),
-            dma((2, 5)), dma((2, 5)), dma((2, 4)), dma((2, 4)),
+            dma((2, REACH, CUTS)), dma((2, REACH, CUTS)),
+            dma((2, REACH, NW)), dma((2, REACH, NW)), dma((2, REACH, NW)), dma((2, REACH, NW)),
+            dma((2, REACH, QB)), dma((2, REACH, QB)),
             dma((8,)), dma((8,)), dma((7,)), dma((7,)),
+            dma((2, 2, NW)), dma((2, 2, NW)), dma((2, 2)), dma((2, 2)),
+            dma((2, 2)), dma((2, 2)), dma((2, 2, NW)), dma((2, 2, NW)),
         ],
         compiler_params=pltpu.CompilerParams(
             collective_id=0, has_side_effects=True, vmem_limit_bytes=56 << 20

time: 86.3 us -> 83.5 us (0.968)
  Pallas kernels: 85.3 us -> 82 us
    pallas_call x1, Pallas kernels: 83.3 us -> 80.1 us  [shards(): pl.pallas_call(kernel, out_shape=outs, in_specs=[hbm] * 7, out_specs=(hbm...]
where the time goes in v3:
time: 83.5 us; the launch traced here: 82.6 us
  Pallas kernels  82 us (98%)
    pallas_call x1, Pallas kernels, shards(): pl.pallas_call(kernel, out_shape=outs, in_specs=[hbm] * 7, out_specs=(hbm...  80.1 us
    pallas_call x1, Pallas kernels, shards(): pl.pallas_call(place, out_shape=outs, in_specs=[vmem] * 4, out_specs=(vme...  1.91 us

profile of v3, /device:TPU:6, one launch (start us, length us, event | category | flops | bytes accessed | tf_op | source)
XLA Modules:
  0.0 82.6 jit_solution(193570390626095873)
XLA Ops:
  0.6 80.1 %shard_map.102 = (bf16[256,512]{1,0:T(8,128)(2,1)}, bf16[4,64,128]{2,1,0:T(8,128)(2,1)}, bf16[4,64,128]{2,1,0:T(8,128)(2,1)}, bf16[448,256]{1,0:T(8,128)(2,1)}) custom-call(bf16[256,512]{1,0:T(8,128)(2,1)} %q_hbm.1, bf16[4,64,128]{2,1,0:T(8,128)(2,1)} %bitcast.9, bf16[4,64,128]{2,1,0:T(8,128)(2,1)} %bitcast.10, bf16[256,512]{1,0:T(8,128)(2,1)} %g_hbm.1, ...), custom_call_target="tpu_custom_call" | custom-call | tf_op jit(solution)/shard_map/pallas_call | solution.py:617
  80.7 1.9 %shard_map.103 = (bf16[256,512]{1,0:T(8,128)(2,1)}, bf16[4,64,128]{2,1,0:T(8,128)(2,1)}, bf16[4,64,128]{2,1,0:T(8,128)(2,1)}, bf16[448,256]{1,0:T(8,128)(2,1)}) custom-call(bf16[256,512]{1,0:T(8,128)(2,1)} %get-tuple-element.12.refs_0_, bf16[4,64,128]{2,1,0:T(8,128)(2,1)} %get-tuple-element.13.refs_1_, bf16[4,64,128]{2,1,0:T(8,128)(2,1)} %get-tuple-element.14.refs_2_, ...), custom_call_target="tpu_custom_call" | custom-call | tf_op jit(solution)/shard_map/pallas_call | solution.py:680

commit v4 on v3

--- a/solution.py
+++ b/solution.py
@@ -213,8 +213,8 @@
             spread_start(t, 1, c)
     req_in.wait()
     for t in range(2):
+        far_hand_out(t)
         hand_out(t, 0)
-        far_hand_out(t)
     for k in range(1, REACH + 1):
         if k < REACH:
             for c in range(CUTS):
@@ -518,6 +518,63 @@
                 if d + 2 <= 7:
                     gate_down(d + 2).start()
 
+    def fetch_sent(t):
+        for r in range(1, REACH):
+
+            @pl.when((y >= r - 1) & (y < NY - 1))
+            def _(r=r):
+                for c in range(CUTS):
+                    spread(t, r, c).wait_send()
+
+        for r in range(REACH):
+
+            @pl.when(y >= r)
+            def _(r=r):
+                def sent(m, c):
+                    fetch(t, r, m).wait_send()
+                    return c
+
+                lax.fori_loop(1, NW, sent, 0)
+
+        for j in range(2):
+
+            @pl.when(y < 2 - j)
+            def _(j=j):
+                def sent(m, c):
+                    far_fetch(t, j, m).wait_send()
+                    return c
+
+                lax.fori_loop(1, NW, sent, 0)
+                far_push(t, j).wait_send()
+
+    def sums_sent(t):
+        for r in range(REACH):
+
+            @pl.when(y >= r)
+            def _(r=r):
+                def sent(m, c):
+                    give(t, r, m).wait_send()
+                    return c
+
+                lax.fori_loop(1, NW, sent, 0)
+                if r > 0:
+                    for j in range(QB):
+                        hop(t, r, j).wait_send()
+
+        for j in range(2):
+
+            @pl.when(y < 2 - j)
+            def _(j=j):
+                def sent(m, c):
+                    far_deal(t, j, m).wait_send()
+                    return c
+
+                lax.fori_loop(1, NW, sent, 0)
+
+            @pl.when(y >= NY - 2 + j)
+            def _(j=j):
+                far_give(t, j).wait_send()
+
     pass_on(1, 4)
     far_relay(1)
     pass_on(0, 5)
@@ -526,10 +583,12 @@
     gate_step(1)
     pass_on(0, 4)
     query(1)
+    fetch_sent(0)
     pass_on(1, 2)
     gate_step(2)
     pass_on(0, 3)
     query(2)
+    fetch_sent(1)
     far_relay(0)
     pass_on(1, 1)
     pass_on(0, 2)
@@ -544,52 +603,14 @@
     gi_ref[...] = dot(gwp[...].astype(jnp.bfloat16), gates, TN).astype(jnp.bfloat16)
     gi_out = pltpu.make_async_copy(gi_ref, gi_hbm, out_s.at[1])
     gi_out.start()
-    finish(0, dk_ref)
-
-    for t in range(2):
-        for r in range(1, REACH):
-
-            @pl.when((y >= r - 1) & (y < NY - 1))
-            def _(t=t, r=r):
-                for c in range(CUTS):
-                    spread(t, r, c).wait_send()
-
-            @pl.when(y >= r)
-            def _(t=t, r=r):
-                for j in range(QB):
-                    hop(t, r, j).wait_send()
-
-        for r in range(REACH):
-
-            @pl.when(y >= r)
-            def _(t=t, r=r):
-                def sent(m, c):
-                    fetch(t, r, m).wait_send()
-                    give(t, r, m).wait_send()
-                    return c
-
-                lax.fori_loop(1, NW, sent, 0)
-
-        for j in range(2):
-
-            @pl.when(y < 2 - j)
-            def _(t=t, j=j):
-                def sent(m, c):
-                    far_fetch(t, j, m).wait_send()
-                    far_deal(t, j, m).wait_send()
-                    return c
-
-                lax.fori_loop(1, NW, sent, 0)
-                far_push(t, j).wait_send()
-
-            @pl.when(y >= NY - 2 + j)
-            def _(t=t, j=j):
-                far_give(t, j).wait_send()
-
+    sums_sent(1)
     for d in range(1, 9):
         gate_up(d).wait_send()
         if d < 8:
             gate_down(d).wait_send()
+    sums_sent(0)
+    finish(0, dk_ref)
+
     dq_out.wait()
     gi_out.wait()
 

time: 83.5 us -> 83.2 us (level)
  no operation moved by 1% of the time
where the time goes in v4:
time: 83.2 us; the launch traced here: 82 us
  Pallas kernels  81.4 us (98%)
    pallas_call x1, Pallas kernels, shards(): pl.pallas_call(kernel, out_shape=outs, in_specs=[hbm] * 7, out_specs=(hbm...  79.5 us
    pallas_call x1, Pallas kernels, shards(): pl.pallas_call(place, out_shape=outs, in_specs=[vmem] * 4, out_specs=(vme...  1.91 us

profile of v4, /device:TPU:6, one launch (start us, length us, event | category | flops | bytes accessed | tf_op | source)
XLA Modules:
  0.0 82.0 jit_solution(139583433290620845)
XLA Ops:
  0.6 79.5 %shard_map.102 = (bf16[256,512]{1,0:T(8,128)(2,1)}, bf16[4,64,128]{2,1,0:T(8,128)(2,1)}, bf16[4,64,128]{2,1,0:T(8,128)(2,1)}, bf16[448,256]{1,0:T(8,128)(2,1)}) custom-call(bf16[256,512]{1,0:T(8,128)(2,1)} %q_hbm.1, bf16[4,64,128]{2,1,0:T(8,128)(2,1)} %bitcast.9, bf16[4,64,128]{2,1,0:T(8,128)(2,1)} %bitcast.10, bf16[256,512]{1,0:T(8,128)(2,1)} %g_hbm.1, ...), custom_call_target="tpu_custom_call" | custom-call | tf_op jit(solution)/shard_map/pallas_call | solution.py:638
  80.1 1.9 %shard_map.103 = (bf16[256,512]{1,0:T(8,128)(2,1)}, bf16[4,64,128]{2,1,0:T(8,128)(2,1)}, bf16[4,64,128]{2,1,0:T(8,128)(2,1)}, bf16[448,256]{1,0:T(8,128)(2,1)}) custom-call(bf16[256,512]{1,0:T(8,128)(2,1)} %get-tuple-element.12.refs_0_, bf16[4,64,128]{2,1,0:T(8,128)(2,1)} %get-tuple-element.13.refs_1_, bf16[4,64,128]{2,1,0:T(8,128)(2,1)} %get-tuple-element.14.refs_2_, ...), custom_call_target="tpu_custom_call" | custom-call | tf_op jit(solution)/shard_map/pallas_call | solution.py:701
